TPU v7x, 32 devices: a whole 2x2x4 slice. The times are simulated.
32 devices in a mesh: pts: 16 (over z, y, x), sub: 2 (over core).
Axes of the slice: x: 2, y: 2, z: 4, core: 2. Of those that a mesh axis runs over, the one named last changes fastest.
Arguments:
- points: bfloat16 [65536, 6], P(('pts', 'sub')), may hold values from -18 to 18
- route: int32 [65536], P(('pts', 'sub')), may hold values from 0 to 4095, as said below
- labels: int32 [65536], P(('pts', 'sub')), may hold values from 0 to 12, as said below
- interp_src: int32 [65536, 3], P(('pts', 'sub')), may hold values from 0 to 1023
- pool_nbr: int32 [16384, 16], P('pts'), may hold values from 0 to 8191, as said below
- sample: int32 [16384], P('pts'), may hold values from 0 to 8191, as said below
- coarse_nbr: int32 [16384, 16], P('pts'), may hold values from 0 to 1023
- owner: int32 [5], replicated, may hold values from 0 to 15, as said below
- step: int32 [1], replicated, may hold values from 2 to 20
- flat: float32 [6909], replicated
- flat_mom: float32 [6909], replicated, may hold values from -9.1552734e-05 to 9.1552734e-05
- flat_sec: float32 [6909], replicated, may hold values from 1.0953302e-10 to 7.667312e-10
- flat_ema: float32 [6909], replicated
- mats: float32 [16, 64, 64], P('pts'), may hold values from -0.75 to 0.75
- mats_mom: float32 [16, 64, 64], P('pts'), may hold values from -9.1552734e-05 to 9.1552734e-05
- mats_sec: float32 [16, 64, 64], P('pts'), may hold values from 1.0953302e-10 to 7.667312e-10
- mats_left: float32 [16, 64, 64], P('pts')
- mats_right: float32 [16, 64, 64], P('pts')
- mats_basis_l: float32 [16, 64, 64], P('pts')
- mats_basis_r: float32 [16, 64, 64], P('pts')
- mats_ema: float32 [16, 64, 64], P('pts'), may hold values from -0.75 to 0.75
Outputs:
- loss: float32 [], replicated
- grad_norm: float32 [], replicated
- flat_new: float32 [6909], replicated
- flat_mom_new: float32 [6909], replicated
- flat_sec_new: float32 [6909], replicated
- flat_ema_new: float32 [6909], replicated
- mats_new: float32 [16, 64, 64], P('pts')
- mats_mom_new: float32 [16, 64, 64], P('pts')
- mats_sec_new: float32 [16, 64, 64], P('pts')
- mats_left_new: float32 [16, 64, 64], P('pts')
- mats_right_new: float32 [16, 64, 64], P('pts')
- mats_basis_l_new: float32 [16, 64, 64], P('pts')
- mats_basis_r_new: float32 [16, 64, 64], P('pts')
- mats_ema_new: float32 [16, 64, 64], P('pts')
Inputs may be any that keep to these rules, and one draw needn't show every extreme that they name: `route`: within one device's rows the values are distinct; value // 256 is the coarse owner along pts and value % 256 the slot. In every draw some device sends 256 rows to one owner, and one owner receives 256 rows from every device. `labels`: every class occurs. `pool_nbr`: each names a received row of the coarse point's owner that some fine point fills. `sample`: each names a received row of the coarse point's owner that some fine point fills. `owner`: distinct slots.
All inputs are finite; a program needn't handle non-finite values.
Results may differ from a plain program's by a relative error of at most 0.0004.
The roundings to bfloat16 on the way count: a program that leaves them out, or rounds other values in their place, can miss the bound.
Values may be sent and summed in bfloat16 or wider, within the bound.
A program may use at most 128 MiB of HBM per device.

v0:
```python
import math

import jax
import jax.numpy as jnp
from jax import lax
from jax.sharding import PartitionSpec as P

C0 = 32
C1 = 64
NEIGH = 16
NCLS = 13
GROUPS = 8


HIGHEST = lax.Precision.HIGHEST
CLIP_NORM = 0.01
BETA_ONE = 0.9
BETA_TWO = 0.95
ADAM_EPS = 1e-08
LEARN_RATE = 0.1
WEIGHT_DECAY = 0.01
EMA_KEEP = 0.9
INTERP_EPS = 0.01
COARSE_NAMES = ("b_down", "w_pos", "b_pos", "w_att1", "b_att1", "w_att2", "b_att2", "w_up", "b_up")


def layout():
    return [
        ("w_stem", (6, C0)),
        ("b_stem", (C0,)),
        ("w_down", (3 + C0, C1)),
        ("b_down", (C1,)),
        ("w_pos", (3, C1)),
        ("b_pos", (C1,)),
        ("w_att1", (C1, GROUPS)),
        ("b_att1", (GROUPS,)),
        ("w_att2", (GROUPS, GROUPS)),
        ("b_att2", (GROUPS,)),
        ("w_up", (C1, C0)),
        ("b_up", (C0,)),
        ("w_skip", (C0, C0)),
        ("w_head", (C0, NCLS)),
        ("b_head", (NCLS,)),
    ]


def unpack(flat):
    parts = {}
    offset = 0
    for entry_name, entry_shape in layout():
        number = math.prod(entry_shape)
        parts[entry_name] = flat[offset : offset + number].reshape(entry_shape)
        offset = offset + number
    return parts


def pack(parts):
    return jnp.concatenate([parts[entry_name].reshape(-1) for entry_name, entry_shape in layout()])


def lowdot(left, right):
    return jnp.einsum("...i,ij->...j", left, right, preferred_element_type=jnp.float32)


def back_prod(grads, weight):
    return jnp.einsum("...j,ij->...i", grads, weight, preferred_element_type=jnp.float32)


def outer_sum(inputs, grads):
    inputs = inputs.reshape(-1, inputs.shape[-1])
    grads = grads.reshape(-1, grads.shape[-1])
    return jnp.dot(inputs.T, grads, preferred_element_type=jnp.float32)


def exact_dot(left, right):
    return jnp.dot(left, right, precision=HIGHEST)


def relu(values):
    return jnp.maximum(values, 0.0)


def spread(rows, route, n_pts, capacity):
    empty = jnp.zeros((n_pts * capacity,) + rows.shape[1:], rows.dtype)
    return empty.at[route].set(rows).reshape((n_pts, capacity) + rows.shape[1:])


def orthonormal(matrix):
    for repeat in range(2):
        gram = exact_dot(matrix.T, matrix)
        factor_low = jnp.linalg.cholesky(gram)
        matrix = lax.linalg.triangular_solve(
            factor_low, matrix, left_side=False, lower=True, transpose_a=True
        )
    return matrix


def soap_update(weight, grad, first, second, left, right, basis_l, basis_r, average, count):
    left_new = BETA_TWO * left + (1.0 - BETA_TWO) * exact_dot(grad, grad.T)
    right_new = BETA_TWO * right + (1.0 - BETA_TWO) * exact_dot(grad.T, grad)
    rotated = exact_dot(exact_dot(basis_l.T, grad), basis_r)
    first_new = BETA_ONE * first + (1.0 - BETA_ONE) * rotated
    second_new = BETA_TWO * second + (1.0 - BETA_TWO) * rotated * rotated
    scaled = (
        first_new
        / (1.0 - BETA_ONE**count)
        / (jnp.sqrt(second_new / (1.0 - BETA_TWO**count)) + ADAM_EPS)
    )
    weight_new = weight - LEARN_RATE * (
        exact_dot(exact_dot(basis_l, scaled), basis_r.T) + WEIGHT_DECAY * weight
    )
    basis_l_new = orthonormal(exact_dot(left_new, basis_l))
    basis_r_new = orthonormal(exact_dot(right_new, basis_r))
    plain = exact_dot(exact_dot(basis_l, first_new), basis_r.T)
    first_out = exact_dot(exact_dot(basis_l_new.T, plain), basis_r_new)
    average_new = EMA_KEEP * average + (1.0 - EMA_KEEP) * weight_new
    return (
        weight_new,
        first_out,
        second_new,
        left_new,
        right_new,
        basis_l_new,
        basis_r_new,
        average_new,
    )


def adam_update(weight, grad, first, second, average, count):
    first_new = BETA_ONE * first + (1.0 - BETA_ONE) * grad
    second_new = BETA_TWO * second + (1.0 - BETA_TWO) * grad * grad
    scaled = (
        first_new
        / (1.0 - BETA_ONE**count)
        / (jnp.sqrt(second_new / (1.0 - BETA_TWO**count)) + ADAM_EPS)
    )
    weight_new = weight - LEARN_RATE * (scaled + WEIGHT_DECAY * weight)
    return (weight_new, first_new, second_new, EMA_KEEP * average + (1.0 - EMA_KEEP) * weight_new)


def local(
    points,
    route,
    labels,
    interp_src,
    pool_nbr,
    sample,
    coarse_nbr,
    owner,
    step,
    flat,
    flat_mom,
    flat_sec,
    flat_ema,
    mats,
    mats_mom,
    mats_sec,
    mats_left,
    mats_right,
    mats_basis_l,
    mats_basis_r,
    mats_ema,
):
    n_pts = lax.axis_size("pts")
    n_sub = lax.axis_size("sub")
    fine_rows = points.shape[0]
    coarse_rows = sample.shape[0]
    capacity = 2 * fine_rows // n_pts
    send_rows = n_pts * capacity
    sub_half = lax.axis_index("sub")
    params = unpack(flat)
    low_params = {
        entry_name: params[entry_name].astype(jnp.bfloat16) for entry_name, entry_shape in layout()
    }
    mine_flag = (owner == lax.axis_index("pts")).astype(jnp.float32)
    mine = mine_flag[:, None, None] * mats[0].astype(jnp.bfloat16).astype(jnp.float32)[None]
    layer_mats = lax.psum(mine, "pts").astype(jnp.bfloat16)
    w_qkv = jnp.concatenate([layer_mats[0], layer_mats[1], layer_mats[2]], 1)
    w_pos2 = layer_mats[3]
    w_out = layer_mats[4]
    w_down = low_params["w_down"]
    xyz = points[:, :3]
    stem_pre = lowdot(points, low_params["w_stem"]) + params["b_stem"]
    stem_low = relu(stem_pre).astype(jnp.bfloat16)
    fine_cat = jnp.concatenate([xyz, stem_low], 1)
    projected = lowdot(fine_cat, w_down).astype(jnp.bfloat16)
    got_rows, got_xyz, got_src = (
        lax.all_to_all(
            spread(projected, route, n_pts, capacity),
            "pts",
            split_axis=0,
            concat_axis=0,
            tiled=True,
        ),
        lax.all_to_all(
            spread(xyz, route, n_pts, capacity), "pts", split_axis=0, concat_axis=0, tiled=True
        ),
        lax.all_to_all(
            spread(interp_src, route, n_pts, capacity),
            "pts",
            split_axis=0,
            concat_axis=0,
            tiled=True,
        ),
    )
    both_rows, both_xyz = (
        lax.all_gather(got_rows[None], "sub", axis=0, tiled=True),
        lax.all_gather(got_xyz[None], "sub", axis=0, tiled=True),
    )
    recv_xyz = both_xyz.reshape(-1, 3)
    recv_proj = both_rows.reshape(-1, C1)
    centre = recv_xyz[sample]
    centre_term = lowdot(centre, w_down[:3])
    pool_in = recv_proj[pool_nbr].astype(jnp.float32) - centre_term[:, None, :] + params["b_down"]
    pooled = jax.nn.logsumexp(pool_in, axis=1)
    pool_wts = jnp.exp(pool_in - pooled[:, None, :])
    pooled_low = pooled.astype(jnp.bfloat16)
    qkv_rows = lowdot(pooled_low, w_qkv)
    queries = qkv_rows[:, :C1]
    key_rows = qkv_rows[:, C1 : 2 * C1]
    value_rows = qkv_rows[:, 2 * C1 :]
    offsets = (
        centre[:, None, :].astype(jnp.float32) - centre[coarse_nbr].astype(jnp.float32)
    ).astype(jnp.bfloat16)
    pos_pre = lowdot(offsets, low_params["w_pos"]) + params["b_pos"]
    pos_low = relu(pos_pre).astype(jnp.bfloat16)
    pos_enc = lowdot(pos_low, w_pos2)
    edge_low = (queries[:, None, :] - key_rows[coarse_nbr] + pos_enc).astype(jnp.bfloat16)
    score_one = lowdot(edge_low, low_params["w_att1"]) + params["b_att1"]
    act_low = relu(score_one).astype(jnp.bfloat16)
    score_two = lowdot(act_low, low_params["w_att2"]) + params["b_att2"]
    attn = jax.nn.softmax(score_two, axis=1)
    carried = (value_rows[coarse_nbr] + pos_enc).reshape(coarse_rows, NEIGH, GROUPS, C1 // GROUPS)
    mixed_low = (
        jnp.sum(attn[..., None] * carried, axis=1).reshape(coarse_rows, C1).astype(jnp.bfloat16)
    )
    block_out = pooled + lowdot(mixed_low, w_out)
    block_low = block_out.astype(jnp.bfloat16)
    coarse_up = lowdot(block_low, low_params["w_up"]) + params["b_up"]
    own_xyz = got_xyz.reshape(-1, 3).astype(jnp.float32)
    own_src = got_src.reshape(-1, 3)
    diffs = own_xyz[:, None, :] - centre[own_src].astype(jnp.float32)
    inverse_d = 1.0 / (jnp.sum(diffs * diffs, axis=2) + INTERP_EPS)
    interp_wts = inverse_d / jnp.sum(inverse_d, axis=1, keepdims=True)
    interp_rows = jnp.sum(interp_wts[..., None] * coarse_up[own_src], axis=1)
    back_rows = lax.all_to_all(
        interp_rows.astype(jnp.bfloat16).reshape(n_pts, capacity, C0),
        "pts",
        split_axis=0,
        concat_axis=0,
        tiled=True,
    )
    fine_interp = back_rows.reshape(-1, C0)[route]
    joined = fine_interp.astype(jnp.float32) + lowdot(stem_low, low_params["w_skip"])
    joined_low = relu(joined).astype(jnp.bfloat16)
    logits = lowdot(joined_low, low_params["w_head"]) + params["b_head"]
    onehot = (labels[:, None] == jnp.arange(NCLS, dtype=jnp.int32)[None, :]).astype(jnp.float32)
    counts = lax.psum(jnp.sum(onehot, axis=0), ("pts", "sub"))
    total_fine = fine_rows * n_pts * n_sub
    class_wts = total_fine / (NCLS * counts)
    row_wts = jnp.sum(onehot * class_wts, axis=1) / total_fine
    lse_rows = jax.nn.logsumexp(logits, axis=1)
    loss_part = jnp.sum(row_wts * (lse_rows - jnp.sum(onehot * logits, axis=1)))
    dlogits = row_wts[:, None] * (jnp.exp(logits - lse_rows[:, None]) - onehot)
    grads = {}
    grads["b_head"] = jnp.sum(dlogits, axis=0)
    dlog_low = dlogits.astype(jnp.bfloat16)
    grads["w_head"] = outer_sum(joined_low, dlog_low)
    dfused_low = (back_prod(dlog_low, low_params["w_head"]) * (joined > 0)).astype(jnp.bfloat16)
    grads["w_skip"] = outer_sum(stem_low, dfused_low)
    dstem = back_prod(dfused_low, low_params["w_skip"])
    up_grads = lax.all_to_all(
        spread(dfused_low, route, n_pts, capacity), "pts", split_axis=0, concat_axis=0, tiled=True
    )
    own_dr = up_grads.reshape(-1, C0).astype(jnp.float32)
    contrib = interp_wts[..., None] * own_dr[:, None, :]
    dcoarse_part = (
        jnp.zeros((coarse_rows, C0), jnp.float32)
        .at[own_src.reshape(-1)]
        .add(contrib.reshape(-1, C0))
    )
    dcoarse = lax.psum(dcoarse_part.astype(jnp.bfloat16), "sub").astype(jnp.float32)
    grads["b_up"] = jnp.sum(dcoarse, axis=0)
    dup_low = dcoarse.astype(jnp.bfloat16)
    grads["w_up"] = outer_sum(block_low, dup_low)
    dblock = back_prod(dup_low, low_params["w_up"])
    dbranch_low = dblock.astype(jnp.bfloat16)
    grad_wout = outer_sum(mixed_low, dbranch_low)
    dmixed = back_prod(dbranch_low, w_out).reshape(coarse_rows, GROUPS, C1 // GROUPS)
    dattn = jnp.sum(dmixed[:, None] * carried, axis=3)
    dcarried = (attn[..., None] * dmixed[:, None]).reshape(coarse_rows, NEIGH, C1)
    dscore_two = attn * (dattn - jnp.sum(attn * dattn, axis=1, keepdims=True))
    grads["b_att2"] = jnp.sum(dscore_two, axis=(0, 1))
    ds2_low = dscore_two.astype(jnp.bfloat16)
    grads["w_att2"] = outer_sum(act_low, ds2_low)
    dscore_one = back_prod(ds2_low, low_params["w_att2"]) * (score_one > 0)
    grads["b_att1"] = jnp.sum(dscore_one, axis=(0, 1))
    ds1_low = dscore_one.astype(jnp.bfloat16)
    grads["w_att1"] = outer_sum(edge_low, ds1_low)
    dedge = back_prod(ds1_low, low_params["w_att1"])
    flat_nbr = coarse_nbr.reshape(-1)
    dqueries = jnp.sum(dedge, axis=1)
    edge_terms = jnp.concatenate([-dedge, dcarried], 2).reshape(-1, 2 * C1)
    dkv = jnp.zeros((coarse_rows, 2 * C1), jnp.float32).at[flat_nbr].add(edge_terms)
    dpos_low = (dedge + dcarried).astype(jnp.bfloat16)
    grad_wpos2 = outer_sum(pos_low, dpos_low)
    dpos_pre = back_prod(dpos_low, w_pos2) * (pos_pre > 0)
    grads["b_pos"] = jnp.sum(dpos_pre, axis=(0, 1))
    grads["w_pos"] = outer_sum(offsets, dpos_pre.astype(jnp.bfloat16))
    dqkv_low = jnp.concatenate([dqueries, dkv], 1).astype(jnp.bfloat16)
    grad_qkv = outer_sum(pooled_low, dqkv_low)
    dpooled = dblock + back_prod(dqkv_low, w_qkv)
    dpool_in = pool_wts * dpooled[:, None, :]
    grads["b_down"] = jnp.sum(dpool_in, axis=(0, 1))
    dcentre_low = (-jnp.sum(dpool_in, axis=1)).astype(jnp.bfloat16)
    grad_centre = jnp.concatenate(
        [outer_sum(centre, dcentre_low), jnp.zeros((C0, C1), jnp.float32)], 0
    )
    drecv_low = (
        jnp.zeros((n_sub * send_rows, C1), jnp.float32)
        .at[pool_nbr.reshape(-1)]
        .add(dpool_in.reshape(-1, C1))
        .astype(jnp.bfloat16)
    )
    own_part = lax.dynamic_slice_in_dim(drecv_low, sub_half * send_rows, send_rows, 0)
    back_proj = lax.all_to_all(
        own_part.reshape(n_pts, capacity, C1), "pts", split_axis=0, concat_axis=0, tiled=True
    )
    dproj = back_proj.reshape(-1, C1)[route]
    grads["w_down"] = outer_sum(fine_cat, dproj) + grad_centre / n_sub
    dstem = dstem + back_prod(dproj, w_down[3:])
    dstem_pre = dstem * (stem_pre > 0)
    grads["b_stem"] = jnp.sum(dstem_pre, axis=0)
    grads["w_stem"] = outer_sum(points, dstem_pre.astype(jnp.bfloat16))
    for coarse_name in COARSE_NAMES:
        grads[coarse_name] = grads[coarse_name] / n_sub
    stacked = jnp.stack(
        [grad_qkv[:, :C1], grad_qkv[:, C1 : 2 * C1], grad_qkv[:, 2 * C1 :], grad_wpos2, grad_wout]
    )
    flat_grad, loss, mats_grad = lax.psum((pack(grads), loss_part, stacked / n_sub), ("pts", "sub"))
    grad_norm = jnp.sqrt(jnp.sum(flat_grad * flat_grad) + jnp.sum(mats_grad * mats_grad))
    factor = jnp.minimum(1.0, CLIP_NORM / grad_norm)
    count = step[0].astype(jnp.float32)
    flat_out = adam_update(flat, flat_grad * factor, flat_mom, flat_sec, flat_ema, count)
    my_grad = jnp.einsum("m,mij->ij", mine_flag, mats_grad, precision=HIGHEST)
    owned = jnp.sum(mine_flag) > 0.5
    results = soap_update(
        mats[0],
        my_grad * factor,
        mats_mom[0],
        mats_sec[0],
        mats_left[0],
        mats_right[0],
        mats_basis_l[0],
        mats_basis_r[0],
        mats_ema[0],
        count,
    )
    placed = [jnp.where(owned, result, 0.0)[None] for result in results]
    return (
        loss,
        grad_norm,
        flat_out[0],
        flat_out[1],
        flat_out[2],
        flat_out[3],
        placed[0],
        placed[1],
        placed[2],
        placed[3],
        placed[4],
        placed[5],
        placed[6],
        placed[7],
    )


def solution(mesh):
    placed = (
        P(("pts", "sub"), None),
        P(("pts", "sub")),
        P(("pts", "sub")),
        P(("pts", "sub"), None),
        P("pts", None),
        P("pts"),
        P("pts", None),
        P(),
        P(),
        P(),
        P(),
        P(),
        P(),
        P("pts", None, None),
        P("pts", None, None),
        P("pts", None, None),
        P("pts", None, None),
        P("pts", None, None),
        P("pts", None, None),
        P("pts", None, None),
        P("pts", None, None),
    )
    return jax.shard_map(
        local,
        mesh=mesh,
        in_specs=placed,
        out_specs=(
            P(),
            P(),
            P(),
            P(),
            P(),
            P(),
            P("pts", None, None),
            P("pts", None, None),
            P("pts", None, None),
            P("pts", None, None),
            P("pts", None, None),
            P("pts", None, None),
            P("pts", None, None),
            P("pts", None, None),
        ),
        check_vma=False,
    )
```

profile of v0, /device:TPU:0, one launch (start us, length us, event | category | flops | bytes accessed | tf_op | source)
XLA Modules:
  0.0 1339.5 jit_solution(3916033277817136556)
XLA Ops:
  9.7 6.1 scatter_custom_fusion
  16.8 8.3 all-to-all-start
  34.5 78.8 %psum.43 = bf16[5,64,64]{1,2,0:T(8,128)(2,1)S(1)} all-reduce(f32[5,64,64]{1,2,0:T(8,128)S(1)} %broadcast_multiply_fusion.1), channel_id=1, replica_groups=mesh['pts'=16,'sub'=2] {'pts'}, use_global_device_ids=true, to_apply=%region_10.0 | all-reduce | flops 20480 | bytes 122880 | tf_op jit(solution)/shard_map/psum | solution.py:177
  115.2 36.8 %psum.42 = f32[13]{0:T(128)S(1)} all-reduce(f32[13]{0:T(128)S(1)} %convert_reduce_fusion), channel_id=1, replica_groups=mesh['pts'=16,'sub'=2] {'pts','sub'}, use_global_device_ids=true, to_apply=%region_1.0 | all-reduce | flops 13 | bytes 104 | tf_op jit(solution)/shard_map/psum | solution.py:258
  162.4 6.1 scatter_custom_fusion.2
  171.6 6.1 scatter_custom_fusion.1
  181.7 6.1 all-to-all-start.1
  187.8 13.4 %all-gather = bf16[32,256,3]{1,0,2:T(8,128)(2,1)S(1)} all-gather(bf16[16,256,3]{1,0,2:T(8,128)(2,1)S(1)} %copy.465), channel_id=2, replica_groups=mesh['pts'=16,'sub'=2] {'sub'}, dimensions={0}, use_global_device_ids=true | all-gather | bytes 73728 | tf_op jit(solution)/shard_map/all_gather | solution.py:208
  202.3 3.2 gather_fusion
  205.6 57.4 %gather_fusion.4 = bf16[16384,3]{1,0:T(8,128)(2,1)} fusion(bf16[1024,3]{1,0:T(8,128)(2,1)S(1)} %gather_fusion, s32[16384]{0:T(1024)S(1)} %broadcast_clamp_fusion), kind=kCustom, calls=%fused_computation.4 | custom fusion | bytes 262144 | tf_op jit(solution)/shard_map/gather | solution.py:223
  263.0 4.8 copy.485
  267.9 3.7 fusion.19
  273.3 7.0 all-to-all-start.2
  282.4 35.9 %gather_fusion.1 = bf16[12288,3]{1,0:T(8,128)(2,1)S(1)} fusion(bf16[1024,3]{1,0:T(8,128)(2,1)S(1)} %gather_fusion, s32[12288]{0:T(1024)S(1)} %broadcast_clamp_fusion.2), kind=kCustom, calls=%fused_computation.1 | custom fusion | bytes 196608 | tf_op jit(solution)/shard_map/gather | solution.py:242
  319.7 9.2 reshape.563
  328.8 4.5 multiply_reduce_fusion.1
  336.1 3.1 reshape_reshape.3
  340.9 3.0 all-gather.4.cloned.1.call-done
  345.9 57.4 %gather_fusion.2 = bf16[16384,64]{1,0:T(8,128)(2,1)} fusion(bf16[8192,64]{1,0:T(8,128)(2,1)S(1)} %bitcast.324, s32[16384]{0:T(1024)S(1)} %copy-done.10), kind=kCustom, calls=%fused_computation.2 | custom fusion | bytes 4259840 | tf_op jit(solution)/shard_map/gather | solution.py:214
  403.3 5.1 add_reduce_fusion
  408.9 7.4 exponential_reduce_fusion
  417.1 54.4 %gather_fusion.3 = f32[16384,64]{1,0:T(8,128)} fusion(f32[1024,64]{1,0:T(8,128)S(1)} %copy.482, s32[16384]{0:T(1024)S(1)} %broadcast_clamp_fusion), kind=kCustom, calls=%fused_computation.3 | custom fusion | bytes 8454144 | tf_op jit(solution)/shard_map/gather | solution.py:228
  471.6 6.9 copy.483
  478.5 6.6 add_convert_fusion
  487.4 54.4 %gather_fusion.5 = f32[16384,64]{1,0:T(8,128)} fusion(f32[1024,64]{1,0:T(8,128)S(1)} %copy.490, s32[16384]{0:T(1024)S(1)} %broadcast_clamp_fusion), kind=kCustom, calls=%fused_computation.5 | custom fusion | bytes 8454144 | tf_op jit(solution)/shard_map/gather | solution.py:233
  541.8 6.8 copy.491
  548.6 4.5 fusion.9
  555.2 41.0 %gather_fusion.6 = f32[12288,32]{1,0:T(8,128)} fusion(f32[1024,32]{1,0:T(8,128)S(1)} %copy.492, s32[12288]{0:T(1024)S(1)} %broadcast_clamp_fusion.2), kind=kCustom, calls=%fused_computation.6 | custom fusion | bytes 3194880 | tf_op jit(solution)/shard_map/gather | solution.py:245
  596.2 10.7 reshape.463
  606.9 24.7 %multiply_reduce_fusion = bf16[4096,32]{1,0:T(8,128)(2,1)} fusion(f32[4096,3,32]{2,1,0:T(4,128)} %reshape.463, f32[4096,3]{1,0:T(8,128)S(1)} %copy-done.4), kind=kLoop, calls=%fused_computation.27 | loop fusion | flops 655360 | bytes 1884160 | tf_op jit(solution)/shard_map/reduce_sum | solution.py:245
  635.5 7.0 all-to-all-start.3
  645.2 2.6 copy.488
  648.8 12.5 mul.265
  661.4 31.4 %mul.283 = f32[16384,64]{0,1:T(8,128)} reshape(f32[1024,16,8,8]{1,0,3,2:T(8,128)} %mul.265) | data formatting | bytes 8388608 | tf_op jit(solution)/shard_map/mul | solution.py:235
  692.8 6.9 copy.510
  701.9 6.2 gather_fusion.7
  710.2 6.4 scatter_custom_fusion.3
  717.7 7.1 all-to-all-start.4
  727.9 6.7 all-to-all-done.4
  735.9 4.3 mul.275
  740.2 10.7 mul.276
  750.9 82.9 %scatter_custom_fusion.4 = f32[1024,32]{1,0:T(8,128)S(1)} fusion(s32[12288]{0:T(1024)} %bitcast.350, f32[12288,32]{1,0:T(8,128)} %mul.276, f32[12288]{0:T(1024)S(1)} %copy-done.39, f32[]{:T(128)} %constant.53.clone.1), kind=kCustom, calls=%fused_computation.34 | custom fusion | flops 786432 | bytes 6472192 | tf_op jit(solution)/shard_map/scatter-add | solution.py:280
  835.2 14.6 %all-reduce.5.cloned.1.call-done = bf16[1024,32]{0,1:T(8,128)(2,1)} async-done(((bf16[1024,32]{0,1:T(8,128)(2,1)}), bf16[1024,32]{0,1:T(8,128)(2,1)}) %all-reduce.5.cloned.1.call-update) | async-done | bytes 65552 | tf_op jit(solution)/shard_map/psum | solution.py:282
  851.0 5.5 fusion.12
  857.4 5.2 fusion.165
  863.7 8.1 copy.508
  871.8 5.8 bitcast_multiply_fusion.1
  877.6 92.2 %scatter_custom_fusion.5 = f32[1024,128]{1,0:T(8,128)S(1)} fusion(s32[16384]{0:T(1024)} %bitcast.349, f32[16384,64]{1,0:T(8,128)} %bitcast_multiply_fusion.1, f32[]{:T(128)} %constant.63.clone.1, f32[16384,64]{1,0:T(8,128)} %bitcast.327, f32[]{:T(128)} %constant.53.clone.1), kind=kCustom, calls=%fused_computation.16 | custom fusion | flops 4194304 | bytes 17302528 | tf_op jit(solution)/shard_map/scatter-add | solution.py:304
  971.0 12.2 fusion.5
  983.3 4.6 bitcast_multiply_fusion
  987.8 89.8 %scatter_custom_fusion.6 = f32[8192,64]{1,0:T(8,128)} fusion(s32[16384]{0:T(1024)} %bitcast.348, f32[16384,64]{1,0:T(8,128)} %bitcast_multiply_fusion, f32[]{:T(128)} %constant.53.clone.1), kind=kCustom, calls=%fused_computation.60 | custom fusion | flops 1048576 | bytes 2097664 | tf_op jit(solution)/shard_map/scatter-add | solution.py:322
  1080.4 6.8 all-to-all-start.5
  1087.6 5.1 fusion.14
  1098.1 120.2 %all-reduce.7.cloned.1.call-done = f32[5,64,64]{2,1,0:T(8,128)} async-done(((f32[5,64,64]{2,1,0:T(8,128)}), f32[5,64,64]{2,1,0:T(8,128)}) %all-reduce.7.cloned.1.call-update) | async-done | bytes 81936 | tf_op jit(solution)/shard_map/psum | solution.py:340
  1220.1 6.2 gather_fusion.8
  1228.1 43.2 %all-reduce.1 = (f32[]{:T(128)}, f32[6909]{0:T(1024)S(1)}) all-reduce(f32[]{:T(128)} %multiply_reduce_fusion.5, f32[6909]{0:T(1024)S(1)} %concatenate.28), channel_id=1, replica_groups=mesh['pts'=16,'sub'=2] {'pts','sub'}, use_global_device_ids=true, to_apply=%region_19.0 | all-reduce | flops 6910 | bytes 55280 | tf_op jit(solution)/shard_map/psum | solution.py:340
  1276.2 5.8 cholesky.74
  1283.3 4.9 custom-call.8
  1288.8 5.8 cholesky.85
  1296.0 4.9 custom-call.9
  1302.8 5.8 cholesky.96
  1310.0 4.9 custom-call.10
  1315.4 5.8 cholesky.107
  1322.6 4.9 custom-call.11
  (401 shorter events, 99.2 us)
Async XLA Ops:
  7.2 1268.2 %copy-start = (f32[1,64,64]{2,1,0:T(8,128)S(1)}, f32[1,64,64]{2,1,0:T(8,128)}, u32[]{:S(2)}) copy-start(f32[1,64,64]{2,1,0:T(8,128)} %param.43) | copy-start | bytes 49156
  7.2 26.5 %copy-start.84 = (s32[1024]{0:T(1024)S(1)}, s32[1024]{0:T(1024)}, u32[]{:S(2)}) copy-start(s32[1024]{0:T(1024)} %param.29) | copy-start | bytes 12292
  7.2 26.5 %copy-start.53 = (f32[1,64,64]{2,1,0:T(8,128)S(1)}, f32[1,64,64]{2,1,0:T(8,128)}, u32[]{:S(2)}) copy-start(f32[1,64,64]{2,1,0:T(8,128)} %param.37) | copy-start | bytes 49156
  7.2 26.6 %copy-start.86 = (s32[5]{0:T(128)S(1)}, s32[5]{0:T(128)}, u32[]{:S(2)}) copy-start(s32[5]{0:T(128)} %param.31) | copy-start | bytes 64
  7.2 107.8 %copy-start.35 = (s32[2048]{0:T(1024)S(1)}, s32[2048]{0:T(1024)}, u32[]{:S(2)}) copy-start(s32[2048]{0:T(1024)} %param.26) | copy-start | bytes 24580
  8.6 163.0 %copy-start.79 = (s32[2048]{0:T(1024)}, s32[2048]{0:T(1024)S(1)}, u32[]{:S(2)}) copy-start(s32[2048]{0:T(1024)S(1)} %get-tuple-element.54) | copy-start | bytes 24580
  9.3 146.2 %copy-start.33 = (bf16[2048,3]{0,1:T(4,128)(2,1)}, bf16[2048,3]{0,1:T(4,128)(2,1)S(1)}, u32[]{:S(2)}) copy-start(bf16[2048,3]{0,1:T(4,128)(2,1)S(1)} %slice.109) | copy-start | bytes 36868
  9.7 145.0 %copy-start.37 = (bf16[2048,6]{0,1:T(8,128)(2,1)S(1)}, bf16[2048,6]{0,1:T(8,128)(2,1)}, u32[]{:S(2)}) copy-start(bf16[2048,6]{0,1:T(8,128)(2,1)} %param.24) | copy-start | bytes 73732
  16.8 165.0 %all-to-all-start = ((bf16[16,256,3]{1,2,0:T(4,128)(2,1)}), bf16[16,256,3]{1,2,0:T(4,128)(2,1)S(1)}, u32[]{:S(2)}, u32[]{:S(2)}) async-start(bf16[16,256,3]{1,2,0:T(4,128)(2,1)} %copy.464), calls=%async_computation | async-start | bytes 65536 | tf_op jit(solution)/shard_map/all_to_all | solution.py:195
  28.7 239.2 %copy-start.81 = (f32[64]{0:T(128)}, f32[64]{0:T(128)S(1)}, u32[]{:S(2)}) copy-start(f32[64]{0:T(128)S(1)} %get-tuple-element.46) | copy-start | bytes 772
  32.8 138.4 %copy-start.66 = (s32[2048,3]{0,1:T(4,128)S(1)}, s32[2048,3]{0,1:T(4,128)}, u32[]{:S(2)}) copy-start(s32[2048,3]{0,1:T(4,128)} %param.27) | copy-start | bytes 73732
  152.2 19.0 %copy-start.59 = (f32[2048]{0:T(1024)}, f32[2048]{0:T(1024)S(1)}, u32[]{:S(2)}) copy-start(f32[2048]{0:T(1024)S(1)} %select_reduce_fusion.1) | copy-start | bytes 24580
  181.7 91.6 %all-to-all-start.1 = ((s32[16,256,3]{1,2,0:T(4,128)}), s32[16,256,3]{1,2,0:T(4,128)S(1)}, u32[]{:S(2)}, u32[]{:S(2)}) async-start(s32[16,256,3]{1,2,0:T(4,128)} %copy.468), calls=%async_computation.1 | async-start | bytes 131072 | tf_op jit(solution)/shard_map/all_to_all | solution.py:198
  205.5 76.9 %copy-start.1 = (bf16[1024,3]{1,0:T(8,128)(2,1)}, bf16[1024,3]{1,0:T(8,128)(2,1)S(1)}, u32[]{:S(2)}) copy-start(bf16[1024,3]{1,0:T(8,128)(2,1)S(1)} %gather_fusion) | copy-start | bytes 18436
  267.8 12.5 copy-start.24
  267.9 13.1 copy-start.62
  273.3 9.1 copy-start.26
  273.3 60.1 %all-to-all-start.2 = ((bf16[16,256,64]{1,2,0:T(8,128)(2,1)}), bf16[16,256,64]{1,2,0:T(8,128)(2,1)}, u32[]{:S(2)}, u32[]{:S(2)}) async-start(bf16[16,256,64]{1,2,0:T(8,128)(2,1)} %copy.472), calls=%async_computation.2 | async-start | bytes 1048576 | tf_op jit(solution)/shard_map/all_to_all | solution.py:188
  280.2 63.6 %all-gather.4.cloned.1.call-start = ((), (), s32[]{:S(2)}) async-start(), calls=%async_computation.8 | async-start | bytes 1572864 | tf_op jit(solution)/shard_map/all_gather | solution.py:207
  319.7 9.2 copy-start.32
  345.9 57.4 %copy-start.8 = (f32[1024,64]{1,0:T(8,128)S(1)}, f32[1024,64]{1,0:T(8,128)}, u32[]{:S(2)}) copy-start(f32[1024,64]{1,0:T(8,128)} %fusion.179) | copy-start | bytes 786436
  345.9 57.4 %copy-start.76 = (f32[64]{0:T(128)S(1)}, f32[64]{0:T(128)}, u32[]{:S(2)}) copy-start(f32[64]{0:T(128)} %get-tuple-element.47) | copy-start | bytes 772
  596.2 10.7 copy-start.4
  635.5 65.0 %all-to-all-start.3 = ((bf16[16,256,32]{1,2,0:T(8,128)(2,1)}), bf16[16,256,32]{1,2,0:T(8,128)(2,1)}, u32[]{:S(2)}, u32[]{:S(2)}) async-start(bf16[16,256,32]{1,2,0:T(8,128)(2,1)} %bitcast.342), calls=%async_computation.3 | async-start | bytes 524288 | tf_op jit(solution)/shard_map/all_to_all | solution.py:246
  692.8 9.2 copy-start.56
  699.7 8.6 copy-start.13
  699.7 8.6 copy-start.57
  699.7 8.9 copy-start.58
  699.7 8.9 copy-start.92
  699.7 9.2 copy-start.36
  699.7 9.2 copy-start.50
  717.7 16.9 %all-to-all-start.4 = ((bf16[16,256,32]{1,2,0:T(8,128)(2,1)}), bf16[16,256,32]{1,2,0:T(8,128)(2,1)}, u32[]{:S(2)}, u32[]{:S(2)}) async-start(bf16[16,256,32]{1,2,0:T(8,128)(2,1)} %copy.501), calls=%async_computation.4 | async-start | bytes 524288 | tf_op jit(solution)/shard_map/all_to_all | solution.py:272
  724.8 125.0 %all-reduce.5.cloned.1.call-start = ((), (), s32[]{:S(2)}) async-start(), calls=%async_computation.6 | async-start | bytes 131072 | tf_op jit(solution)/shard_map/psum | solution.py:282
  740.2 10.7 copy-start.39
  750.9 83.7 %copy-start.60 = (f32[2048]{0:T(1024)S(1)}, f32[2048]{0:T(1024)}, u32[]{:S(2)}) copy-start(f32[2048]{0:T(1024)} %copy-done.59) | copy-start | bytes 24580
  750.9 98.9 %copy-start.49 = (bf16[64,32]{1,0:T(8,128)(2,1)S(1)}, bf16[64,32]{1,0:T(8,128)(2,1)}, u32[]{:S(2)}) copy-start(bf16[64,32]{1,0:T(8,128)(2,1)} %convert_element_type.198) | copy-start | bytes 12292
  750.9 99.9 %copy-start.64 = (bf16[1,64,64]{2,1,0:T(8,128)(2,1)S(1)}, bf16[1,64,64]{2,1,0:T(8,128)(2,1)}, u32[]{:S(2)}) copy-start(bf16[1,64,64]{2,1,0:T(8,128)(2,1)} %copy.505) | copy-start | bytes 24580
  877.6 92.2 %copy-start.29 = (bf16[1024,64]{0,1:T(8,128)(2,1)S(1)}, bf16[1024,64]{0,1:T(8,128)(2,1)}, u32[]{:S(2)}) copy-start(bf16[1024,64]{0,1:T(8,128)(2,1)} %get-tuple-element.28) | copy-start | bytes 393220
  877.6 92.4 %copy-start.43 = (bf16[64,64]{0,1:T(8,128)(2,1)S(1)}, bf16[64,64]{0,1:T(8,128)(2,1)}, u32[]{:S(2)}) copy-start(bf16[64,64]{0,1:T(8,128)(2,1)} %get-tuple-element.37) | copy-start | bytes 24580
  877.6 92.4 %copy-start.45 = (bf16[64,64]{0,1:T(8,128)(2,1)S(1)}, bf16[64,64]{0,1:T(8,128)(2,1)}, u32[]{:S(2)}) copy-start(bf16[64,64]{0,1:T(8,128)(2,1)} %get-tuple-element.38) | copy-start | bytes 24580
  877.6 92.4 %copy-start.47 = (bf16[64,64]{0,1:T(8,128)(2,1)S(1)}, bf16[64,64]{0,1:T(8,128)(2,1)}, u32[]{:S(2)}) copy-start(bf16[64,64]{0,1:T(8,128)(2,1)} %get-tuple-element.39) | copy-start | bytes 24580
  877.6 93.4 %copy-start.77 = (f32[64]{0:T(128)S(1)}, f32[64]{0:T(128)}, u32[]{:S(2)}) copy-start(f32[64]{0:T(128)} %get-tuple-element.47) | copy-start | bytes 772
  987.8 99.5 %copy-start.2 = (bf16[1024,3]{1,0:T(8,128)(2,1)S(1)}, bf16[1024,3]{1,0:T(8,128)(2,1)}, u32[]{:S(2)}) copy-start(bf16[1024,3]{1,0:T(8,128)(2,1)} %copy-done.1) | copy-start | bytes 18436
  987.8 99.8 %copy-start.51 = (u16[1024,64]{0,1:T(8,128)(2,1)S(1)}, u16[1024,64]{0,1:T(8,128)(2,1)}, u32[]{:S(2)}) copy-start(u16[1024,64]{0,1:T(8,128)(2,1)} %get-tuple-element.68) | copy-start | bytes 393220
  1080.4 139.1 %all-to-all-start.5 = ((bf16[16,256,64]{1,2,0:T(8,128)(2,1)}), bf16[16,256,64]{1,2,0:T(8,128)(2,1)S(1)}, u32[]{:S(2)}, u32[]{:S(2)}) async-start(bf16[16,256,64]{1,2,0:T(8,128)(2,1)} %copy.514), calls=%async_computation.5 | async-start | bytes 1048576 | tf_op jit(solution)/shard_map/all_to_all | solution.py:326
  1087.2 131.0 %all-reduce.7.cloned.1.call-start = ((), (), s32[]{:S(2)}) async-start(), calls=%async_computation.7 | async-start | bytes 327680 | tf_op jit(solution)/shard_map/psum | solution.py:340
  1094.2 124.0 %copy-start.87 = (s32[5]{0:T(128)S(1)}, s32[5]{0:T(128)}, u32[]{:S(2)}) copy-start(s32[5]{0:T(128)} %param.31) | copy-start | bytes 64
  1097.5 128.8 %copy-start.22 = (f32[2048,32]{0,1:T(8,128)S(1)}, f32[2048,32]{0,1:T(8,128)}, u32[]{:S(2)}) copy-start(f32[2048,32]{0,1:T(8,128)} %get-tuple-element.56) | copy-start | bytes 786436
  1097.5 128.8 %copy-start.23 = (f32[2048,32]{0,1:T(8,128)S(1)}, f32[2048,32]{0,1:T(8,128)}, u32[]{:S(2)}) copy-start(f32[2048,32]{0,1:T(8,128)} %fusion.186) | copy-start | bytes 786436
  1097.5 128.8 %copy-start.65 = (bf16[32,64]{1,0:T(8,128)(2,1)S(1)}, bf16[32,64]{1,0:T(8,128)(2,1)}, u32[]{:S(2)}) copy-start(bf16[32,64]{1,0:T(8,128)(2,1)} %slice.136) | copy-start | bytes 12292
  1097.5 129.2 %copy-start.38 = (bf16[2048,6]{0,1:T(8,128)(2,1)S(1)}, bf16[2048,6]{0,1:T(8,128)(2,1)}, u32[]{:S(2)}) copy-start(bf16[2048,6]{0,1:T(8,128)(2,1)} %param.24) | copy-start | bytes 73732
  1097.5 129.4 %copy-start.14 = (bf16[2048,32]{0,1:T(8,128)(2,1)S(1)}, bf16[2048,32]{0,1:T(8,128)(2,1)}, u32[]{:S(2)}) copy-start(bf16[2048,32]{0,1:T(8,128)(2,1)} %copy-done.12) | copy-start | bytes 393220
  1097.5 129.4 %copy-start.34 = (bf16[2048,3]{0,1:T(4,128)(2,1)S(1)}, bf16[2048,3]{0,1:T(4,128)(2,1)}, u32[]{:S(2)}) copy-start(bf16[2048,3]{0,1:T(4,128)(2,1)} %copy-done.33) | copy-start | bytes 36868
  1219.5 53.8 %copy-start.31 = (f32[1,64,64]{2,1,0:T(8,128)S(1)}, f32[1,64,64]{2,1,0:T(8,128)}, u32[]{:S(2)}) copy-start(f32[1,64,64]{2,1,0:T(8,128)} %param.42) | copy-start | bytes 49156
  1219.5 54.0 %copy-start.67 = (f32[1,64,64]{2,1,0:T(8,128)S(1)}, f32[1,64,64]{2,1,0:T(8,128)}, u32[]{:S(2)}) copy-start(f32[1,64,64]{2,1,0:T(8,128)} %param.40) | copy-start | bytes 49156
  1219.5 54.4 %copy-start.68 = (f32[1,64,64]{2,1,0:T(8,128)S(1)}, f32[1,64,64]{2,1,0:T(8,128)}, u32[]{:S(2)}) copy-start(f32[1,64,64]{2,1,0:T(8,128)} %param.41) | copy-start | bytes 49156
  1220.1 81.1 %copy-start.70 = (f32[1,64,64]{2,1,0:T(8,128)S(1)}, f32[1,64,64]{2,1,0:T(8,128)}, u32[]{:S(2)}) copy-start(f32[1,64,64]{2,1,0:T(8,128)} %param.38) | copy-start | bytes 49156
  1220.1 109.1 %copy-start.69 = (f32[1,64,64]{2,1,0:T(8,128)S(1)}, f32[1,64,64]{2,1,0:T(8,128)}, u32[]{:S(2)}) copy-start(f32[1,64,64]{2,1,0:T(8,128)} %param.39) | copy-start | bytes 49156
  1220.1 110.0 %copy-start.54 = (f32[1,64,64]{2,1,0:T(8,128)S(1)}, f32[1,64,64]{2,1,0:T(8,128)}, u32[]{:S(2)}) copy-start(f32[1,64,64]{2,1,0:T(8,128)} %param.37) | copy-start | bytes 49156
  1220.1 110.0 %copy-start.71 = (f32[1,64,64]{2,1,0:T(8,128)S(1)}, f32[1,64,64]{2,1,0:T(8,128)}, u32[]{:S(2)}) copy-start(f32[1,64,64]{2,1,0:T(8,128)} %param.44) | copy-start | bytes 49156
  1226.3 104.7 %copy-start.55 = (f32[6909]{0:T(1024)S(1)}, f32[6909]{0:T(1024)}, u32[]{:S(2)}) copy-start(f32[6909]{0:T(1024)} %param.33) | copy-start | bytes 82912
  1226.3 104.7 %copy-start.72 = (f32[6909]{0:T(1024)S(1)}, f32[6909]{0:T(1024)}, u32[]{:S(2)}) copy-start(f32[6909]{0:T(1024)} %param.36) | copy-start | bytes 82912
  1226.3 104.7 %copy-start.73 = (f32[6909]{0:T(1024)S(1)}, f32[6909]{0:T(1024)}, u32[]{:S(2)}) copy-start(f32[6909]{0:T(1024)} %param.35) | copy-start | bytes 82912
  1226.3 104.7 %copy-start.74 = (f32[6909]{0:T(1024)S(1)}, f32[6909]{0:T(1024)}, u32[]{:S(2)}) copy-start(f32[6909]{0:T(1024)} %param.34) | copy-start | bytes 82912
  (38 other events, 185.2 us)
Sparse Core Ops, SparseCore 0:
  333.6 10.2 all-gather.3
  834.7 15.0 all-reduce.4
  1095.0 123.1 all-reduce.6
where the time goes:
time: 1350 us; the launch traced here: 1340 us
  local copies, waits for them, and re-layouts  511 us (38%)
  other arithmetic  407 us (30%)
  blocking collectives  172 us (13%)
  waiting for transfers between devices  144 us (11%)
  matrix products  42.4 us (3%)
  starting transfers between devices  42.3 us (3%)
  between operations  19.8 us (1%)
    psum x1, waiting for transfers between devices, local(): lax.psum((pack(grads), loss_part, stacked / n_sub), ('pts', 'sub'))  120 us
    scatter-add x1, other arithmetic, local(): jnp.zeros((coarse_rows, 2 * C1), jnp.float32).at[flat_nbr].add(edge_terms)  92.2 us
    scatter-add x1, other arithmetic, local(): drecv_low = jnp.zeros((n_sub * send_rows, C1), jnp.float32).at[pool_nbr.r...  89.8 us
    scatter-add x1, other arithmetic, local(): dcoarse_part = jnp.zeros((coarse_rows, C0), jnp.float32).at[own_src.resha...  82.9 us
    psum x1, blocking collectives, local(): layer_mats = lax.psum(mine, 'pts').astype(jnp.bfloat16)  78.8 us
    gather x2, local copies, waits for them, and re-layouts, local(): key_rows[coarse_nbr]  61.3 us
    gather x2, local copies, waits for them, and re-layouts, local(): value_rows[coarse_nbr] + pos_enc  61.2 us
    gather x1, local copies, waits for them, and re-layouts, local(): centre[coarse_nbr].astype(jnp.float32)  57.4 us
  transfers between devices with their start and end apart: 9, of which 4 were waited for; matrix products, arithmetic and copies ran while one was open for 18% of the time, Pallas kernels for 0%

commit v1 on v0

v1 whole, which is shorter than its diff:
```python
import functools
import math

import jax
import jax.numpy as jnp
from jax import lax
from jax.experimental import pallas as pl
from jax.experimental.pallas import tpu as pltpu
from jax.sharding import PartitionSpec as P

C0 = 32
C1 = 64
NEIGH = 16
NCLS = 13
GROUPS = 8
NMATS = 5

HIGHEST = lax.Precision.HIGHEST
CLIP_NORM = 0.01
BETA_ONE = 0.9
BETA_TWO = 0.95
ADAM_EPS = 1e-08
LEARN_RATE = 0.1
WEIGHT_DECAY = 0.01
EMA_KEEP = 0.9
INTERP_EPS = 0.01

F32 = jnp.float32
BF16 = jnp.bfloat16
I32 = jnp.int32
MESH = pl.DeviceIdType.MESH
VMEM = pltpu.VMEM

LANES = 128
FLAT_ROWS = 64
LOW_B = 256
CH = 80
NEG = -1e30


def offsets():
    shapes = [
        ("w_stem", (6, C0)),
        ("b_stem", (C0,)),
        ("w_down", (3 + C0, C1)),
        ("b_down", (C1,)),
        ("w_pos", (3, C1)),
        ("b_pos", (C1,)),
        ("w_att1", (C1, GROUPS)),
        ("b_att1", (GROUPS,)),
        ("w_att2", (GROUPS, GROUPS)),
        ("b_att2", (GROUPS,)),
        ("w_up", (C1, C0)),
        ("b_up", (C0,)),
        ("w_skip", (C0, C0)),
        ("w_head", (C0, NCLS)),
        ("b_head", (NCLS,)),
    ]
    found = {}
    total = 0
    for name, shape in shapes:
        found[name] = total
        total += math.prod(shape)
    return found, total


OFF, FLAT = offsets()


def dot(left, right):
    return lax.dot_general(left, right, (((1,), (0,)), ((), ())), preferred_element_type=F32)


def dot_nt(left, right):
    return lax.dot_general(left, right, (((1,), (1,)), ((), ())), preferred_element_type=F32)


def exact(left, right, dims=((1,), (0,))):
    return lax.dot_general(
        left, right, (dims, ((), ())), precision=HIGHEST, preferred_element_type=F32
    )


def relu(values):
    return jnp.maximum(values, 0.0)


def rows_of(count, length):
    return lax.broadcasted_iota(I32, (count, length), 0)


def lanes_of(count, length):
    return lax.broadcasted_iota(I32, (count, length), 1)


def onehot(low, count):
    hit = rows_of(count, low.shape[1]) == low
    return jnp.where(hit, 1.0, 0.0).astype(BF16)


def pick(spread, high, parts):
    each = spread.shape[0] // parts
    found = spread[0:each]
    for part in range(1, parts):
        found = jnp.where(high == part, spread[part * each : (part + 1) * each], found)
    return found


def place(values, high, parts):
    return jnp.concatenate(
        [jnp.where(high == part, values, 0.0) for part in range(parts)], 0
    ).astype(BF16)


def unpack(flat_ref, out_ref, offset, rows, width, at):
    stride = LANES // width if LANES % width == 0 else rows
    for first in range(min(stride, rows)):
        count = (rows - first + stride - 1) // stride
        padded = -(-count // 8) * 8
        line, lane = divmod(offset + first * width, LANES)
        values = flat_ref[line : line + padded, :]
        if lane:
            values = pltpu.roll(values, LANES - lane, 1)
        if lane + width > LANES:
            following = pltpu.roll(flat_ref[line + 1 : line + 1 + padded, :], LANES - lane, 1)
            values = jnp.where(lanes_of(padded, LANES) < LANES - lane, values, following)
        values = jnp.where(lanes_of(padded, LANES) < width, values, 0.0)
        if count == 1:
            out_ref[at + first : at + first + 1, :] = values[0:1]
        else:
            out_ref[pl.ds(at + first, count, stride=stride), :] = values[0:count]


def pack(out_ref, base, source_ref, row, lane_from, offset, rows, width):
    stride = LANES // width if LANES % width == 0 else rows
    for first in range(min(stride, rows)):
        count = (rows - first + stride - 1) // stride
        line, lane = divmod(offset + first * width, LANES)
        if count == 1:
            values = source_ref[row + first : row + first + 1, :]
        else:
            values = source_ref[pl.ds(row + first, count, stride=stride), :]
        shift = (lane - lane_from) % LANES
        padded = -(-count // 8) * 8
        if padded != count:
            values = jnp.concatenate([values, jnp.zeros((padded - count, LANES), F32)], 0)
        if shift:
            values = pltpu.roll(values, shift, 1)
        values = values[0:count]
        at = lanes_of(count, LANES)
        here = jnp.where((at >= lane) & (at < lane + width), values, 0.0)
        out_ref[base + line : base + line + count, :] += here
        if lane + width > LANES:
            there = jnp.where(at < lane + width - LANES, values, 0.0)
            out_ref[base + line + 1 : base + line + 1 + count, :] += there


def main_kernel(
    n_pts,
    n_sub,
    pts_ref,
    route_ref,
    labels_ref,
    src_ref,
    pool_ref,
    sample_ref,
    cnbr_ref,
    owner_ref,
    flat_ref,
    mats_ref,
    out_ref,
    data,
    sacc,
    sendb,
    recv,
    matmine,
    matall,
    tabb,
    cen,
    pin,
    cat,
    pooled_ref,
    rsum_ref,
    ctab,
    btab,
    est,
    ohs,
    car,
    sc,
    mixed_ref,
    blk_ref,
    slot,
    dcp,
    dcr,
    dkp,
    dkr,
    wst,
    wd,
    wp,
    w1,
    w2,
    wu,
    wsk,
    wh,
    bias,
    ga,
    gb,
    gc,
    gd,
    ge,
    gbuf,
    gsib,
    ghalf,
    gsh,
    gfull,
    a2a_send,
    a2a_recv,
    mat_send,
    mat_recv,
    red_send,
    red_recv,
    gat_send,
    gat_recv,
    sib_send,
    sib_recv,
):
    fine = route_ref.shape[1]
    coarse = sample_ref.shape[1]
    cap = sendb.shape[2]
    slots = n_pts * cap
    half = coarse // n_sub
    sources = n_sub * n_pts
    parts = coarse // LOW_B
    my_parts = parts // n_sub
    shift = cap.bit_length() - 1
    low_shift = LOW_B.bit_length() - 1
    span = 512
    me = lax.axis_index("pts")
    sub = lax.axis_index("sub")
    half_at = pl.multiple_of(sub * half, half)

    barrier = pltpu.get_barrier_semaphore()

    def greet(step, carry):
        peer = lax.rem(me + step, n_pts)
        pl.semaphore_signal(barrier, inc=1, device_id={"pts": peer}, device_id_type=MESH)
        return carry

    lax.fori_loop(1, n_pts, greet, 0)
    pl.semaphore_signal(barrier, inc=1, device_id={"sub": 1 - sub}, device_id_type=MESH)

    def sibling(number, source, target):
        return pltpu.make_async_remote_copy(
            src_ref=source,
            dst_ref=target,
            send_sem=sib_send.at[number],
            recv_sem=sib_recv.at[number],
            device_id={"sub": 1 - sub},
            device_id_type=MESH,
        )

    data[0:6, :] = pts_ref[...].astype(F32)
    data[6:8, :] = jnp.zeros((2, fine), F32)
    source_rows = src_ref[...]
    data[8:11, :] = lax.shift_right_logical(source_rows, 5).astype(F32)
    data[11:14, :] = (source_rows & 31).astype(F32)
    data[14:15, :] = (labels_ref[...] + 1).astype(F32)
    data[15:16, :] = jnp.zeros((1, fine), F32)
    sacc[...] = jnp.zeros_like(sacc)
    counts = jnp.zeros((16, 32), F32)
    for chunk in range(fine // span):
        lanes = slice(chunk * span, (chunk + 1) * span)
        route = route_ref[:, lanes]
        high = lax.shift_right_logical(route, shift)
        spread = place(data[:, lanes], high, n_pts)
        sacc[...] += dot_nt(spread, onehot(route & (cap - 1), cap))
        classes = onehot(labels_ref[:, lanes], 16)
        counts = counts + dot_nt(jnp.ones((16, span), BF16), jnp.concatenate([classes, classes], 0))
    count_high = jnp.floor(counts * (1.0 / 128.0))
    count_low = counts - 128.0 * count_high
    digits = jnp.where(lanes_of(16, 32) < 16, count_low, count_high)
    digits = jnp.where(rows_of(16, 32) == 15, digits, 0.0)
    data[:, 0:cap] = jnp.zeros((16, cap), F32)
    data[:, 0:32] = digits
    sendb[...] = (sacc[...].reshape(n_pts, 16, cap) + data[:, 0:cap][None]).astype(BF16)
    matrix = mats_ref[...]
    matmine[...] = jnp.concatenate([matrix[0:32], matrix[32:64]], 1).astype(BF16)

    pl.semaphore_wait(barrier, n_pts)

    def block_copy(peer, index):
        return pltpu.make_async_remote_copy(
            src_ref=sendb.at[peer],
            dst_ref=recv.at[sub * n_pts + index],
            send_sem=a2a_send.at[peer],
            recv_sem=a2a_recv.at[index],
            device_id={"pts": peer},
            device_id_type=MESH,
        )

    def mat_copy(peer, index):
        return pltpu.make_async_remote_copy(
            src_ref=matmine,
            dst_ref=matall.at[index],
            send_sem=mat_send.at[peer],
            recv_sem=mat_recv.at[index],
            device_id={"pts": peer},
            device_id_type=MESH,
        )

    def send_blocks(step, carry):
        block_copy(lax.rem(me + step, n_pts), me).start()
        return carry

    def send_mats(step, carry):
        mat_copy(lax.rem(me + step, n_pts), me).start()
        return carry

    lax.fori_loop(1, n_pts, send_blocks, 0)
    lax.fori_loop(1, n_pts, send_mats, 0)
    recv[sub * n_pts + me] = sendb[me]
    matall[me] = matmine[...]

    for ref in (wst, wd, wp, w1, w2, wu, wsk, wh, bias):
        ref[...] = jnp.zeros_like(ref)
    unpack(flat_ref, wst, OFF["w_stem"], 6, C0, 0)
    unpack(flat_ref, wd, OFF["w_down"], 3, C1, 0)
    unpack(flat_ref, wd, OFF["w_down"] + 3 * C1, C0, C1, 16)
    unpack(flat_ref, wp, OFF["w_pos"], 3, C1, 8)
    unpack(flat_ref, w1, OFF["w_att1"], C1, GROUPS, 0)
    unpack(flat_ref, w2, OFF["w_att2"], GROUPS, GROUPS, 0)
    unpack(flat_ref, wu, OFF["w_up"], C1, C0, 0)
    unpack(flat_ref, wsk, OFF["w_skip"], C0, C0, 0)
    unpack(flat_ref, wh, OFF["w_head"], C0, NCLS, 0)
    names = ("b_stem", "b_down", "b_pos", "b_att1", "b_att2", "b_up", "b_head")
    widths = (C0, C1, C1, GROUPS, GROUPS, C0, NCLS)
    for position, (name, width) in enumerate(zip(names, widths)):
        unpack(flat_ref, bias, OFF[name], 1, width, position)
    columns = bias[...].T
    b_stem = columns[0:C0, 0:1]
    b_down = columns[0:C1, 1:2]
    b_pos = columns[0:C1, 2:3]
    b_att1 = columns[0:GROUPS, 3:4]
    b_att2 = columns[0:GROUPS, 4:5]
    b_up = columns[0:C0, 5:6]
    b_head = jnp.where(rows_of(16, 1) < NCLS, columns[0:16, 6:7], NEG)
    w_stem_t = wst[...].T[0:C0, 0:16].astype(BF16)
    w_down_t = wd[...].T[0:C1, 0:48].astype(BF16)
    w_pos_t = wp[...].T[0:C1, 0:16].astype(BF16)
    w_att1_t = w1[...].T[0:GROUPS, 0:C1].astype(BF16)
    w_att2_t = w2[...].T[0:GROUPS, 0:16].astype(BF16)
    w_up_t = wu[...].T[0:C0, 0:C1].astype(BF16)
    w_skip_t = wsk[...].T[0:C0, 0:C0].astype(BF16)
    w_head_t = wh[...].T[0:16, 0:C0].astype(BF16)
    w_down_stem = wd[16:48, 0:C1].astype(BF16)
    w_att1 = w1[0:C1, 0:16].astype(BF16)
    w_att2 = w2[0:GROUPS, 0:16].astype(BF16)
    w_up = wu[0:C1, 0:C0].astype(BF16)
    w_skip = wsk[0:C0, 0:C0].astype(BF16)
    w_head = wh[0:C0, 0:16].astype(BF16)

    def wait_blocks(step, carry):
        peer = lax.rem(me + step, n_pts)
        block_copy(peer, peer).wait_recv()
        return carry

    lax.fori_loop(1, n_pts, wait_blocks, 0)
    mine = recv.at[pl.ds(sub * n_pts, n_pts)]
    forward = sibling(0, mine, mine)
    forward.start()
    for source in range(n_pts):
        slot[:, source * cap : (source + 1) * cap] = recv[sub * n_pts + source].astype(F32)
    forward.wait_recv()

    table = recv[...].astype(F32)[:, 0:8, :].reshape(sources * 8, cap)
    ones_row = (rows_of(sources * 8, cap) & 7) == 7
    tabb[...] = jnp.where(ones_row, 1.0, table).astype(BF16)
    count_row = jnp.sum(recv[...].astype(F32)[:, 8:16, :], axis=0)[7:8, 0:32]
    count_at = jnp.broadcast_to(count_row, (16, 32))
    low_hit = lanes_of(16, 32) == rows_of(16, 32)
    high_hit = lanes_of(16, 32) == rows_of(16, 32) + 16
    class_counts = jnp.sum(
        jnp.where(low_hit, count_at, 0.0) + jnp.where(high_hit, 128.0 * count_at, 0.0),
        axis=1,
        keepdims=True,
    )
    total_fine = float(fine * n_pts * n_sub)
    class_w = jnp.where(rows_of(16, 1) < NCLS, total_fine / (NCLS * class_counts), 0.0)

    def gather_points(index):
        hot = onehot(index & (cap - 1), cap)
        return pick(dot(tabb[...], hot), lax.shift_right_logical(index, shift), sources)

    zeros8 = jnp.zeros((8, span), F32)
    for chunk in range(coarse // span):
        lanes = slice(chunk * span, (chunk + 1) * span)
        found = gather_points(sample_ref[:, lanes])
        cen[:, lanes] = jnp.where(rows_of(8, span) < 6, found, 0.0)
    centre = cen[:, pl.ds(half_at, half)]
    centre_low = jnp.concatenate([centre, zeros8], 0).astype(BF16)
    w_xyz_t = jnp.where(lanes_of(C1, 16) < 3, wd[...].T[0:C1, 0:16], 0.0).astype(BF16)
    centre_term = dot(w_xyz_t, centre_low)

    def pool_step(k, most):
        found = gather_points(pool_ref[pl.ds(k, 1), pl.ds(half_at, half)])
        low = jnp.concatenate([found, zeros8], 0).astype(BF16)
        stem = relu(dot(w_stem_t, low) + b_stem)
        joined = jnp.concatenate([found, zeros8, stem], 0).astype(BF16)
        cat[k] = joined
        projected = dot(w_down_t, joined).astype(BF16).astype(F32)
        value = projected - centre_term + b_down
        pin[k] = value
        return jnp.maximum(most, value)

    most = lax.fori_loop(0, NEIGH, pool_step, jnp.full((C1, half), -jnp.inf, F32))

    def exp_step(k, total):
        value = jnp.exp(pin[k] - most)
        pin[k] = value
        return total + value

    total = lax.fori_loop(0, NEIGH, exp_step, jnp.zeros((C1, half), F32))
    pooled = most + jnp.log(total)
    pooled_ref[...] = pooled
    rsum_ref[...] = 1.0 / total

    def table_rows(values, target):
        for part in range(my_parts):
            lanes = slice(part * LOW_B, (part + 1) * LOW_B)
            stacked = jnp.concatenate(
                [values[:, lanes], centre[:, lanes], jnp.zeros((8, LOW_B), F32)], 0
            )
            target[sub * my_parts + part] = stacked.astype(BF16)

    table_rows(pooled, ctab)
    my_ctab = ctab.at[pl.ds(sub * my_parts, my_parts)]
    give_pooled = sibling(1, my_ctab, my_ctab)
    give_pooled.start()

    def wait_mats(step, carry):
        peer = lax.rem(me + step, n_pts)
        mat_copy(peer, peer).wait_recv()
        return carry

    lax.fori_loop(1, n_pts, wait_mats, 0)

    def layer(position):
        folded = matall[owner_ref[position]].astype(F32)
        return jnp.concatenate([folded[:, 0:C1], folded[:, C1 : 2 * C1]], 0)

    w_qkv32 = jnp.concatenate([layer(0), layer(1), layer(2)], 1)
    w_qkv = w_qkv32.astype(BF16)
    w_query_t = w_qkv32[:, 0:C1].T.astype(BF16)
    w_kv_t = jnp.concatenate([w_qkv32[:, C1 : 2 * C1].T, w_qkv32[:, 2 * C1 :].T], 0).astype(BF16)
    w_pos2_32 = layer(3)
    w_pos2 = w_pos2_32.astype(BF16)
    w_pos2_t = w_pos2_32.T.astype(BF16)
    w_out_32 = layer(4)
    w_out = w_out_32.astype(BF16)
    w_out_t = w_out_32.T.astype(BF16)
    pooled_low = pooled.astype(BF16)
    queries = dot(w_query_t, pooled_low)
    give_pooled.wait_recv()

    def expand(values):
        return jnp.concatenate(
            [jnp.broadcast_to(values[g : g + 1], (8, values.shape[1])) for g in range(GROUPS)], 0
        )

    def attend(k, most):
        index = cnbr_ref[pl.ds(k, 1), pl.ds(half_at, half)]
        high = lax.shift_right_logical(index, low_shift)
        hot = onehot(index & (LOW_B - 1), LOW_B)
        ohs[k] = hot
        found = pick(dot(ctab[...].reshape(parts * CH, LOW_B), hot), high, parts)
        near = found[0:C1].astype(BF16)
        rows = dot(w_kv_t, near)
        offset = jnp.where(rows_of(8, half) == 7, 1.0, centre - found[C1 : C1 + 8])
        off_low = jnp.concatenate([zeros8, offset], 0).astype(BF16)
        pos_low = relu(dot(w_pos_t, off_low) + b_pos).astype(BF16)
        pos_enc = dot(w_pos2_t, pos_low)
        edge_low = (queries - rows[0:C1] + pos_enc).astype(BF16)
        act = relu(dot(w_att1_t, edge_low) + b_att1)
        act_off = jnp.concatenate([act, offset], 0).astype(BF16)
        score = dot(w_att2_t, act_off) + b_att2
        est[k, 0:64, :] = edge_low
        est[k, 64:128, :] = pos_low
        est[k, 128:144, :] = act_off
        car[k] = rows[C1 : 2 * C1] + pos_enc
        sc[k] = score
        return jnp.maximum(most, score)

    top = lax.fori_loop(0, NEIGH, attend, jnp.full((GROUPS, half), -jnp.inf, F32))

    def weigh(k, total):
        value = jnp.exp(sc[k] - top)
        sc[k] = value
        return total + value

    scale = 1.0 / lax.fori_loop(0, NEIGH, weigh, jnp.zeros((GROUPS, half), F32))

    def mix(k, total):
        weight = sc[k] * scale
        sc[k] = weight
        return total + expand(weight) * car[k]

    mixed = lax.fori_loop(0, NEIGH, mix, jnp.zeros((C1, half), F32))
    mixed_ref[...] = mixed
    block = pooled_ref[...] + dot(w_out_t, mixed.astype(BF16))
    blk_ref[...] = block
    table_rows(block, btab)
    my_btab = btab.at[pl.ds(sub * my_parts, my_parts)]
    give_block = sibling(2, my_btab, my_btab)
    give_block.start()
    give_block.wait_recv()

    ga[...] = jnp.zeros_like(ga)
    dcp[...] = jnp.zeros_like(dcp)

    def fine_step(step, loss):
        at = pl.multiple_of(step * span, span)
        rows = slot[:, pl.ds(at, span)]
        points = rows[0:8]
        source = (32.0 * rows[8:11] + rows[11:14]).astype(I32)
        label = rows[14:15].astype(I32)
        hots = []
        highs = []
        ups = []
        inverses = []
        for i in range(3):
            index = source[i : i + 1]
            high = lax.shift_right_logical(index, low_shift)
            hot = onehot(index & (LOW_B - 1), LOW_B)
            found = pick(dot(btab[...].reshape(parts * CH, LOW_B), hot), high, parts)
            ups.append(dot(w_up_t, found[0:C1].astype(BF16)) + b_up)
            diff = jnp.where(rows_of(8, span) < 3, points - found[C1 : C1 + 8], 0.0)
            inverses.append(1.0 / (jnp.sum(diff * diff, axis=0, keepdims=True) + INTERP_EPS))
            hots.append(hot)
            highs.append(high)
        norm = inverses[0] + inverses[1] + inverses[2]
        weights = [inverse / norm for inverse in inverses]
        interp = weights[0] * ups[0] + weights[1] * ups[1] + weights[2] * ups[2]
        interp = interp.astype(BF16).astype(F32)
        ones = jnp.where(rows_of(8, span) == 7, 1.0, points)
        points_low = jnp.concatenate([ones, zeros8], 0).astype(BF16)
        stem_pre = dot(w_stem_t, points_low) + b_stem
        stem_low = relu(stem_pre).astype(BF16)
        joined = interp + dot(w_skip_t, stem_low)
        joined_low = relu(joined).astype(BF16)
        logits = dot(w_head_t, joined_low) + b_head
        hit = jnp.where(rows_of(16, span) + 1 == label, 1.0, 0.0)
        row_w = jnp.sum(hit * class_w, axis=0, keepdims=True) * (1.0 / total_fine)
        peak = jnp.max(logits, axis=0, keepdims=True)
        lse = peak + jnp.log(jnp.sum(jnp.exp(logits - peak), axis=0, keepdims=True))
        loss = loss + row_w * (lse - jnp.sum(hit * logits, axis=0, keepdims=True))
        dlog_low = (row_w * (jnp.exp(logits - lse) - hit)).astype(BF16)
        dfused_low = jnp.where(joined > 0, dot(w_head, dlog_low), 0.0).astype(BF16)
        dfused = dfused_low.astype(F32)
        dstem = jnp.where(stem_pre > 0, dot(w_skip, dfused_low), 0.0).astype(BF16)
        inputs = jnp.concatenate([points_low, stem_low, joined_low], 0)
        grads = jnp.concatenate([dfused_low, dstem, dlog_low], 0)
        ga[:, 0:80] += dot_nt(inputs, grads)
        spread = jnp.concatenate(
            [place(weights[i] * dfused, highs[i], parts) for i in range(3)], 1
        )
        dcp[...] += dot_nt(spread, jnp.concatenate(hots, 1)).reshape(parts, C0, LOW_B)
        return loss

    loss = lax.fori_loop(0, slots // span, fine_step, jnp.zeros((1, span), F32))

    other = (1 - sub) * my_parts
    own = sub * my_parts
    give_dup = sibling(3, dcp.at[pl.ds(other, my_parts)], dcr)
    give_dup.start()
    give_dup.wait_recv()

    def own_half(partial, received):
        return jnp.concatenate(
            [partial[own + part] + received[part] for part in range(my_parts)], 1
        )

    dup_low = own_half(dcp, dcr).astype(BF16)
    dblock = dot(w_up, dup_low)
    dbranch_low = dblock.astype(BF16)
    dmixed = dot(w_out, dbranch_low)
    inputs = jnp.concatenate(
        [blk_ref[...].astype(BF16), mixed_ref[...].astype(BF16), jnp.ones((16, half), BF16)], 0
    )
    grads = jnp.concatenate([dup_low, jnp.zeros((C0, half), BF16), dbranch_low], 0)
    gd[...] = dot_nt(inputs, grads)

    def group_sum(values):
        return jnp.concatenate(
            [
                jnp.sum(values[8 * g : 8 * g + 8], axis=0, keepdims=True)
                for g in range(GROUPS)
            ],
            0,
        )

    centred = group_sum(dmixed * mixed_ref[...])
    gc[...] = jnp.zeros_like(gc)
    ge[...] = jnp.zeros_like(ge)
    dkp[...] = jnp.zeros_like(dkp)

    def attend_back(k, total):
        weight = sc[k]
        act_off = est[k, 128:144, :].astype(F32)
        pos_low = est[k, 64:128, :]
        ds2 = weight * (group_sum(dmixed * car[k]) - centred)
        ds2_low = jnp.concatenate([ds2, zeros8], 0).astype(BF16)
        ds1 = jnp.where(act_off[0:8] > 0, dot(w_att2, ds2_low), 0.0)
        ds1_low = jnp.concatenate([ds1, zeros8], 0).astype(BF16)
        ds1_kept = ds1_low.astype(F32)[0:8]
        dedge = dot(w_att1, ds1_low)
        dcarried = expand(weight) * dmixed
        dpos_low = (dedge + dcarried).astype(BF16)
        dpos_pre = jnp.where(pos_low.astype(F32) > 0, dot(w_pos2, dpos_low), 0.0).astype(BF16)
        small = jnp.concatenate([ds1, ds2], 0).astype(BF16)
        result = dot_nt(est[k], jnp.concatenate([dpos_pre, dpos_low, small], 0))
        gc[...] += result[:, 0:128]
        ge[:, 0:16] += result[:, 128:144]
        index = cnbr_ref[pl.ds(k, 1), pl.ds(half_at, half)]
        high = lax.shift_right_logical(index, low_shift)
        spread = place(jnp.concatenate([dcarried, ds1_kept], 0), high, parts)
        dkp[...] += dot_nt(spread, ohs[k]).reshape(parts, C1 + 8, LOW_B)
        return total + ds1_kept

    ds1_total = lax.fori_loop(0, NEIGH, attend_back, jnp.zeros((GROUPS, half), F32))
    give_dkv = sibling(4, dkp.at[pl.ds(other, my_parts)], dkr)
    give_dkv.start()
    give_dkv.wait_recv()
    dkv = own_half(dkp, dkr)
    w_att1_exact = w1[0:C1, 0:16].astype(BF16).astype(F32)[:, 0:8]
    dqueries = exact(w_att1_exact, ds1_total)
    dkeys = -exact(w_att1_exact, dkv[C1 : C1 + 8])
    dqkv_low = jnp.concatenate([dqueries, dkeys, dkv[0:C1]], 0).astype(BF16)
    gbuf[...] = jnp.zeros_like(gbuf)
    gbuf[0:64, :] = dot_nt(pooled_ref[...].astype(BF16), dqkv_low[0:128])
    gbuf[64:128, 0:64] = dot_nt(pooled_ref[...].astype(BF16), dqkv_low[128:192])
    dpooled = dblock + dot(w_qkv, dqkv_low)

    gb[...] = jnp.zeros_like(gb)
    gb[0:16, 0:C1] = dot_nt(centre_low, (-dpooled).astype(BF16))
    dscaled = dpooled * rsum_ref[...]

    def pool_back(k, carry):
        dpin = (pin[k] * dscaled).astype(BF16)
        joined = cat[k]
        dstem = jnp.where(joined[16:48].astype(F32) > 0, dot(w_down_stem, dpin), 0.0).astype(BF16)
        gb[:, 0:96] += dot_nt(joined, jnp.concatenate([dpin, dstem], 0))
        return carry

    lax.fori_loop(0, NEIGH, pool_back, 0)

    left = lanes_of(64, LANES) < 64
    gd_out = gd[64:128, :]
    gbuf[64:128, :] = jnp.where(left, gbuf[64:128, :], gc[64:128, :])
    gbuf[128:160, :] = jnp.where(left[0:32], pltpu.roll(gd_out[0:32], 64, 1), gd_out[32:64])
    base = 160
    pack(gbuf, base, ga, 0, 32, OFF["w_stem"], 6, C0)
    pack(gbuf, base, gb, 0, 64, OFF["w_stem"], 6, C0)
    pack(gbuf, base, ga, 7, 32, OFF["b_stem"], 1, C0)
    pack(gbuf, base, gb, 7, 64, OFF["b_stem"], 1, C0)
    pack(gbuf, base, gb, 0, 0, OFF["w_down"], 3, C1)
    pack(gbuf, base, gb, 16, 0, OFF["w_down"] + 3 * C1, C0, C1)
    pack(gbuf, base, gb, 7, 0, OFF["b_down"], 1, C1)
    pack(gbuf, base, gc, 136, 0, OFF["w_pos"], 3, C1)
    pack(gbuf, base, gc, 143, 0, OFF["b_pos"], 1, C1)
    pack(gbuf, base, ge, 0, 0, OFF["w_att1"], C1, GROUPS)
    pack(gbuf, base, ge, 143, 0, OFF["b_att1"], 1, GROUPS)
    pack(gbuf, base, ge, 128, 8, OFF["w_att2"], GROUPS, GROUPS)
    pack(gbuf, base, ge, 143, 8, OFF["b_att2"], 1, GROUPS)
    pack(gbuf, base, gd, 0, 0, OFF["w_up"], C1, C0)
    pack(gbuf, base, gd, 128, 0, OFF["b_up"], 1, C0)
    pack(gbuf, base, ga, 16, 0, OFF["w_skip"], C0, C0)
    pack(gbuf, base, ga, 48, 64, OFF["w_head"], C0, NCLS)
    pack(gbuf, base, ga, 7, 64, OFF["b_head"], 1, NCLS)
    loss_sum = jnp.sum(loss, axis=1, keepdims=True)
    line, lane = divmod(FLAT, LANES)
    at_loss = lanes_of(1, LANES) == lane
    gbuf[base + line : base + line + 1, :] += jnp.where(at_loss, loss_sum, 0.0)

    rows = gbuf.shape[0] // n_sub
    shards = rows // 8
    give_grad = sibling(5, gbuf.at[pl.ds(pl.multiple_of((1 - sub) * rows, rows), rows)], gsib)
    give_grad.start()
    give_grad.wait_recv()
    ghalf[...] = gbuf[pl.ds(pl.multiple_of(sub * rows, rows), rows), :] + gsib[...]
    mine_at = pl.multiple_of(sub * rows + me * 8, 8)

    def shard_copy(peer, index):
        return pltpu.make_async_remote_copy(
            src_ref=ghalf.at[pl.ds(pl.multiple_of(peer * 8, 8), 8)],
            dst_ref=gsh.at[index],
            send_sem=red_send.at[peer],
            recv_sem=red_recv.at[index],
            device_id={"pts": peer},
            device_id_type=MESH,
        )

    def sum_copy(peer, index):
        at = pl.multiple_of(sub * rows + index * 8, 8)
        return pltpu.make_async_remote_copy(
            src_ref=gfull.at[pl.ds(at, 8)],
            dst_ref=gfull.at[pl.ds(at, 8)],
            send_sem=gat_send.at[peer],
            recv_sem=gat_recv.at[index],
            device_id={"pts": peer},
            device_id_type=MESH,
        )

    holds = None if n_pts <= shards else me < shards

    def when(condition, run):
        if condition is None:
            run()
        else:
            pl.when(condition)(run)

    def each_peer(run, limited):
        def body(step, carry):
            peer = lax.rem(me + step, n_pts)
            when(None if holds is None or not limited else peer < shards, lambda: run(peer))
            return carry

        lax.fori_loop(1, n_pts, body, 0)

    each_peer(lambda peer: shard_copy(peer, me).start(), True)

    def reduce():
        gsh[me] = ghalf[pl.ds(pl.multiple_of(me * 8, 8), 8), :]
        each_peer(lambda peer: shard_copy(peer, peer).wait_recv(), False)
        gfull[pl.ds(mine_at, 8), :] = jnp.sum(gsh[...], axis=0)
        each_peer(lambda peer: sum_copy(peer, me).start(), False)

    when(holds, reduce)
    each_peer(lambda peer: sum_copy(peer, peer).wait_recv(), True)
    half_rows = gfull.at[pl.ds(pl.multiple_of(sub * rows, rows), rows)]
    give_full = sibling(6, half_rows, half_rows)
    give_full.start()

    each_peer(lambda peer: block_copy(peer, me).wait_send(), False)
    each_peer(lambda peer: mat_copy(peer, me).wait_send(), False)
    each_peer(lambda peer: shard_copy(peer, me).wait_send(), True)
    when(holds, lambda: each_peer(lambda peer: sum_copy(peer, me).wait_send(), False))
    for copy in (forward, give_pooled, give_block, give_dup, give_dkv, give_grad, give_full):
        copy.wait_send()
    give_full.wait_recv()
    out_ref[...] = gfull[...]


def orthonormal_pair(matrix):
    size = matrix.shape[0]
    lane = lanes_of(size, 2 * size)
    left = lane < size
    column = lanes_of(1, 2 * size)
    left_row = column < size
    place_row = jnp.where(left_row, column, column - size)
    for repeat in range(2):
        for j in range(size):
            pivot = jnp.where(left, matrix[:, j : j + 1], matrix[:, size + j : size + j + 1])
            products = jnp.sum(pivot * matrix, axis=0, keepdims=True)
            norms = jnp.where(
                left_row, products[:, j : j + 1], products[:, size + j : size + j + 1]
            )
            factor = jnp.where(place_row > j, products / norms, 0.0)
            matrix = matrix - pivot * factor
        matrix = matrix * lax.rsqrt(jnp.sum(matrix * matrix, axis=0, keepdims=True))
    return matrix


def soap_kernel(
    grads_ref,
    owner_ref,
    step_ref,
    weight_ref,
    first_ref,
    second_ref,
    left_ref,
    right_ref,
    basis_l_ref,
    basis_r_ref,
    average_ref,
    weight_out,
    first_out,
    second_out,
    left_out,
    right_out,
    basis_l_out,
    basis_r_out,
    average_out,
    flat_out,
    scalars_out,
):
    me = lax.axis_index("pts")
    grads = grads_ref[...]
    line, lane = divmod(FLAT, LANES)
    place_row = rows_of(256, LANES)
    at_loss = (place_row == 160 + line) & (lanes_of(256, LANES) == lane)
    loss = jnp.sum(jnp.where(at_loss, grads, 0.0))
    cleaned = jnp.where(at_loss, 0.0, grads)
    squares = jnp.sum(jnp.sum(cleaned * cleaned, axis=0, keepdims=True), axis=1, keepdims=True)
    norm = jnp.sqrt(squares)
    factor = jnp.minimum(1.0, CLIP_NORM / norm)
    flat_out[...] = cleaned[160:216] * factor
    at = lanes_of(8, LANES)
    scalars_out[...] = jnp.where(at == 0, loss, jnp.where(at == 1, norm, 0.0))
    folded = cleaned[128:160]
    stacked = [
        cleaned[0:64, 0:64],
        cleaned[0:64, 64:128],
        cleaned[64:128, 0:64],
        cleaned[64:128, 64:128],
        jnp.concatenate([folded[:, 0:64], folded[:, 64:128]], 0),
    ]
    grad = jnp.zeros((C1, C1), F32)
    owned = 0.0
    for position in range(NMATS):
        flag = jnp.where(owner_ref[position] == me, 1.0, 0.0)
        grad = grad + flag * stacked[position]
        owned = owned + flag
    grad = grad * factor
    count = jnp.full((1, 1), step_ref[0].astype(F32), F32)
    one_scale = 1.0 - jnp.exp(count * math.log(BETA_ONE))
    two_scale = 1.0 - jnp.exp(count * math.log(BETA_TWO))
    basis_l = basis_l_ref[...]
    basis_r = basis_r_ref[...]
    left_new = BETA_TWO * left_ref[...] + (1.0 - BETA_TWO) * exact(grad, grad, ((1,), (1,)))
    right_new = BETA_TWO * right_ref[...] + (1.0 - BETA_TWO) * exact(grad, grad, ((0,), (0,)))
    both = orthonormal_pair(
        jnp.concatenate([exact(left_new, basis_l), exact(right_new, basis_r)], 1)
    )
    basis_l_new = both[:, 0:C1]
    basis_r_new = both[:, C1 : 2 * C1]
    rotated = exact(exact(basis_l, grad, ((0,), (0,))), basis_r)
    first_new = BETA_ONE * first_ref[...] + (1.0 - BETA_ONE) * rotated
    second_new = BETA_TWO * second_ref[...] + (1.0 - BETA_TWO) * rotated * rotated
    scaled = first_new / one_scale / (jnp.sqrt(second_new / two_scale) + ADAM_EPS)
    weight = weight_ref[...]
    weight_new = weight - LEARN_RATE * (
        exact(exact(basis_l, scaled), basis_r, ((1,), (1,))) + WEIGHT_DECAY * weight
    )
    plain = exact(exact(basis_l, first_new), basis_r, ((1,), (1,)))
    first_rotated = exact(exact(basis_l_new, plain, ((0,), (0,))), basis_r_new)
    average_new = EMA_KEEP * average_ref[...] + (1.0 - EMA_KEEP) * weight_new
    held = owned > 0.5
    weight_out[...] = jnp.where(held, weight_new, 0.0)
    first_out[...] = jnp.where(held, first_rotated, 0.0)
    second_out[...] = jnp.where(held, second_new, 0.0)
    left_out[...] = jnp.where(held, left_new, 0.0)
    right_out[...] = jnp.where(held, right_new, 0.0)
    basis_l_out[...] = jnp.where(held, basis_l_new, 0.0)
    basis_r_out[...] = jnp.where(held, basis_r_new, 0.0)
    average_out[...] = jnp.where(held, average_new, 0.0)


def adam_update(weight, grad, first, second, average, count):
    first_new = BETA_ONE * first + (1.0 - BETA_ONE) * grad
    second_new = BETA_TWO * second + (1.0 - BETA_TWO) * grad * grad
    scaled = (
        first_new
        / (1.0 - BETA_ONE**count)
        / (jnp.sqrt(second_new / (1.0 - BETA_TWO**count)) + ADAM_EPS)
    )
    weight_new = weight - LEARN_RATE * (scaled + WEIGHT_DECAY * weight)
    return (weight_new, first_new, second_new, EMA_KEEP * average + (1.0 - EMA_KEEP) * weight_new)


def local(
    points,
    route,
    labels,
    interp_src,
    pool_nbr,
    sample,
    coarse_nbr,
    owner,
    step,
    flat,
    flat_mom,
    flat_sec,
    flat_ema,
    mats,
    mats_mom,
    mats_sec,
    mats_left,
    mats_right,
    mats_basis_l,
    mats_basis_r,
    mats_ema,
):
    n_pts = lax.axis_size("pts")
    n_sub = lax.axis_size("sub")
    fine = points.shape[0]
    coarse = sample.shape[0]
    cap = n_sub * fine // n_pts
    slots = n_pts * cap
    sources = n_sub * n_pts
    half = coarse // n_sub
    parts = coarse // LOW_B
    my_parts = parts // n_sub
    flat2 = jnp.pad(flat, (0, FLAT_ROWS * LANES - FLAT)).reshape(FLAT_ROWS, LANES)
    vmem = pl.BlockSpec(memory_space=pltpu.VMEM)
    smem = pl.BlockSpec(memory_space=pltpu.SMEM)
    dma = pltpu.SemaphoreType.DMA
    scratch = [
        VMEM((16, fine), F32),
        VMEM((n_pts * 16, cap), F32),
        VMEM((n_pts, 16, cap), BF16),
        VMEM((sources, 16, cap), BF16),
        VMEM((32, LANES), BF16),
        VMEM((n_pts, 32, LANES), BF16),
        VMEM((sources * 8, cap), BF16),
        VMEM((8, coarse), F32),
        VMEM((NEIGH, C1, half), F32),
        VMEM((NEIGH, 48, half), BF16),
        VMEM((C1, half), F32),
        VMEM((C1, half), F32),
        VMEM((parts, CH, LOW_B), BF16),
        VMEM((parts, CH, LOW_B), BF16),
        VMEM((NEIGH, 144, half), BF16),
        VMEM((NEIGH, LOW_B, half), BF16),
        VMEM((NEIGH, C1, half), F32),
        VMEM((NEIGH, GROUPS, half), F32),
        VMEM((C1, half), F32),
        VMEM((C1, half), F32),
        VMEM((16, slots), F32),
        VMEM((parts, C0, LOW_B), F32),
        VMEM((my_parts, C0, LOW_B), F32),
        VMEM((parts, C1 + 8, LOW_B), F32),
        VMEM((my_parts, C1 + 8, LOW_B), F32),
        VMEM((LANES, LANES), F32),
        VMEM((LANES, LANES), F32),
        VMEM((LANES, LANES), F32),
        VMEM((LANES, LANES), F32),
        VMEM((LANES, LANES), F32),
        VMEM((LANES, LANES), F32),
        VMEM((LANES, LANES), F32),
        VMEM((LANES, LANES), F32),
        VMEM((LANES, LANES), F32),
        VMEM((80, LANES), F32),
        VMEM((48, LANES), F32),
        VMEM((144, LANES), F32),
        VMEM((144, LANES), F32),
        VMEM((144, LANES), F32),
        VMEM((256, LANES), F32),
        VMEM((128, LANES), F32),
        VMEM((128, LANES), F32),
        VMEM((n_pts, 8, LANES), F32),
        VMEM((256, LANES), F32),
        dma((n_pts,)),
        dma((n_pts,)),
        dma((n_pts,)),
        dma((n_pts,)),
        dma((n_pts,)),
        dma((n_pts,)),
        dma((n_pts,)),
        dma((n_pts,)),
        dma((8,)),
        dma((8,)),
    ]
    reduced = pl.pallas_call(
        functools.partial(main_kernel, n_pts, n_sub),
        out_shape=jax.ShapeDtypeStruct((256, LANES), F32),
        in_specs=[vmem] * 7 + [smem] + [vmem] * 2,
        out_specs=vmem,
        scratch_shapes=scratch,
        compiler_params=pltpu.CompilerParams(
            collective_id=0, has_side_effects=True, vmem_limit_bytes=48 * 1024 * 1024
        ),
    )(
        points.T,
        route.reshape(1, fine),
        labels.reshape(1, fine),
        interp_src.T,
        pool_nbr.T,
        sample.reshape(1, coarse),
        coarse_nbr.T,
        owner,
        flat2,
        mats[0],
    )
    square = jax.ShapeDtypeStruct((C1, C1), F32)
    results = pl.pallas_call(
        soap_kernel,
        out_shape=[square] * 8
        + [
            jax.ShapeDtypeStruct((56, LANES), F32),
            jax.ShapeDtypeStruct((8, LANES), F32),
        ],
        in_specs=[vmem] + [smem] * 2 + [vmem] * 8,
        out_specs=[vmem] * 10,
    )(
        reduced,
        owner,
        step,
        mats[0],
        mats_mom[0],
        mats_sec[0],
        mats_left[0],
        mats_right[0],
        mats_basis_l[0],
        mats_basis_r[0],
        mats_ema[0],
    )
    flat_grad = results[8].reshape(-1)[:FLAT]
    count = step[0].astype(F32)
    flat_out = adam_update(flat, flat_grad, flat_mom, flat_sec, flat_ema, count)
    return (results[9][0, 0], results[9][0, 1]) + flat_out + tuple(
        result[None] for result in results[:8]
    )


def solution(mesh):
    placed = (
        P(("pts", "sub"), None),
        P(("pts", "sub")),
        P(("pts", "sub")),
        P(("pts", "sub"), None),
        P("pts", None),
        P("pts"),
        P("pts", None),
        P(),
        P(),
        P(),
        P(),
        P(),
        P(),
    ) + (P("pts", None, None),) * 8
    return jax.shard_map(
        local,
        mesh=mesh,
        in_specs=placed,
        out_specs=(P(),) * 6 + (P("pts", None, None),) * 8,
        check_vma=False,
    )
```

time: 1350 us -> 122 us (0.09)
  local copies, waits for them, and re-layouts: 511 us -> 7.29 us
  other arithmetic: 407 us -> 1.4 us
  blocking collectives: 172 us -> 0 us
  waiting for transfers between devices: 144 us -> 0 us
  Pallas kernels: 0 us -> 111 us
  matrix products: 42.4 us -> 0 us
  starting transfers between devices: 42.3 us -> 0 us
  between operations: 19.8 us -> 1.5 us
    gather x14 -> x0, local copies, waits for them, and re-layouts: 341 us -> none  [the longest x2 61.3 us: local(): key_rows[coarse_nbr]]
    scatter-add x3 -> x0, other arithmetic: 265 us -> none  [the longest x1 92.2 us: local(): jnp.zeros((coarse_rows, 2 * C1), jnp.float32).at[flat_nbr].add(edge_terms)]
    psum x3 -> x0, blocking collectives: 159 us -> none  [the longest x1 78.8 us: local(): layer_mats = lax.psum(mine, 'pts').astype(jnp.bfloat16)]
    psum x2 -> x0, waiting for transfers between devices: 135 us -> none  [the longest x1 120 us: local(): lax.psum((pack(grads), loss_part, stacked / n_sub), ('pts', 'sub'))]
    pallas_call x0 -> x2, Pallas kernels: none -> 111 us  [the longest x1 85.8 us: local(): pl.pallas_call(functools.partial(main_kernel, n_pts, n_sub), out_shape=ja...]
    mul x6 -> x0, local copies, waits for them, and re-layouts: 65.9 us -> none  [the longest x3 50.8 us: local(): attn[..., None] * carried]
    reduce_sum x19 -> x0, other arithmetic: 63.5 us -> none  [the longest x1 24.7 us: local(): interp_rows = jnp.sum(interp_wts[..., None] * coarse_up[own_src], axis=1)]
    another operation x22 -> x0, other arithmetic: 49.1 us -> none  [the longest x12 26.1 us: orthonormal(): factor_low = jnp.linalg.cholesky(gram)]
  transfers between devices with their start and end apart: 9 -> 0, of which waited for: 4 -> 0; matrix products, arithmetic and copies ran while one was open for 18% -> 0% of each run, Pallas kernels for 0% -> 0%
where the time goes in v1:
time: 122 us; the launch traced here: 121 us
  Pallas kernels  111 us (91%)
  local copies, waits for them, and re-layouts  7.29 us (6%)
  between operations  1.5 us (1%)
  other arithmetic  1.4 us (1%)
    pallas_call x1, Pallas kernels, local(): pl.pallas_call(functools.partial(main_kernel, n_pts, n_sub), out_shape=ja...  85.8 us
    pallas_call x1, Pallas kernels, local(): pl.pallas_call(soap_kernel, out_shape=[square] * 8 + [jax.ShapeDtypeStruc...  25.4 us
    unnamed x28, local copies, waits for them, and re-layouts  5.19 us

profile of v1, /device:TPU:0, one launch (start us, length us, event | category | flops | bytes accessed | tf_op | source)
XLA Modules:
  0.0 121.4 jit_solution(12235948073380923171)
XLA Ops:
  0.6 0.0 copy-start.1
  0.7 0.0 copy-start.4
  0.7 0.8 pad_bitcast_fusion.flat_ref
  1.4 0.0 copy-start.6
  1.4 0.0 copy-start.9
  1.4 0.0 copy-done.1
  1.4 0.0 copy-done.4
  1.4 0.7 copy-done.6
  2.1 0.0 copy-done.9
  2.1 0.0 copy-start.2
  2.1 0.8 copy-done.2
  3.0 0.0 copy-start.3
  3.0 0.8 copy-done.3
  3.8 0.0 copy-start.5
  3.8 0.8 copy-done.5
  4.6 0.0 copy-start.7
  4.6 0.7 copy-done.7
  5.3 0.0 copy-start.8
  5.3 0.7 copy-done.8
  6.0 85.8 %shard_map.308.grads_ref = f32[256,128]{1,0:T(8,128)S(1)} custom-call(bf16[6,2048]{1,0:T(8,128)(2,1)S(1)} %bitcast.34, s32[1,2048]{1,0:T(1,128)S(1)} %bitcast.36, s32[1,2048]{1,0:T(1,128)S(1)} %bitcast.37, s32[3,2048]{1,0:T(4,128)S(1)} %bitcast.35, s32[16,1024]{1,0:T(8,128)S(1)} %bitcast.32, s32[1,1024]{1,0:T(1,128)S(1)} %bitcast.38, ...), custom_call_target="tpu_custom_call" | custom-call | tf_op jit(solution)/shard_map/pallas_call | solution.py:963
  91.8 0.0 copy-start
  91.8 0.6 copy-done
  93.1 0.0 copy-start.10
  93.1 0.0 copy-start.11
  93.1 0.0 copy-start.12
  93.1 0.0 copy-start.13
  93.2 25.4 %shard_map.309 = (f32[64,64]{1,0:T(8,128)}, f32[64,64]{1,0:T(8,128)}, f32[64,64]{1,0:T(8,128)}, f32[64,64]{1,0:T(8,128)}, f32[64,64]{1,0:T(8,128)}, /*index=5*/f...) custom-call(f32[256,128]{1,0:T(8,128)} %copy-done, s32[5]{0:T(128)} %owner_ref.3, ...), custom_call_target="tpu_custom_call" | custom-call | tf_op jit(solution)/shard_map/pallas_call | solution.py:985
  118.6 0.0 copy-done.10
  118.6 0.0 copy-done.11
  118.7 0.0 copy-done.12
  118.7 0.0 copy-done.13
  118.7 1.4 %multiply_add_fusion = (f32[6909]{0:T(1024)}, f32[6909]{0:T(1024)}, f32[6909]{0:T(1024)}, f32[6909]{0:T(1024)}) fusion(f32[6909]{0:T(1024)S(1)} %copy-done.11, f32[6909]{0:T(1024)S(1)} %copy-done.10, f32[]{:T(128)} %bitcast.20, f32[]{:T(128)} %bitcast.19, f32[7168]{0:T(1024)} %bitcast.46, f32[6909]{0:T(1024)S(1)} %copy-done.12, f32[6909]{0:T(1024)S(1)} %copy-done.13), kind=kLoop, calls=%fused_computation.3 | loop fusion | flops 124362 | bytes 248732 | tf_op jit(solution)/shard_map/add | solution.py:867
  120.1 1.3 %fusion.2 = (f32[1,1]{1,0:T(1,128)}, f32[1,1]{1,0:T(1,128)}) fusion(f32[8,128]{1,0:T(8,128)} %get-tuple-element.24), kind=kLoop, calls=%fused_computation.6 | loop fusion | bytes 16 | tf_op jit(solution)/shard_map/slice | solution.py:1010
Async XLA Ops:
  0.6 0.8 copy-start.1
  0.7 0.8 copy-start.4
  1.4 0.7 copy-start.6
  1.4 0.7 copy-start.9
  2.1 0.8 copy-start.2
  3.0 0.8 copy-start.3
  3.8 0.8 copy-start.5
  4.6 0.7 copy-start.7
  5.3 0.7 copy-start.8
  91.8 0.7 copy-start
  93.1 25.5 %copy-start.10 = (f32[6909]{0:T(1024)S(1)}, f32[6909]{0:T(1024)}, u32[]{:S(2)}) copy-start(f32[6909]{0:T(1024)} %param.30) | copy-start | bytes 82912
  93.1 25.5 %copy-start.11 = (f32[6909]{0:T(1024)S(1)}, f32[6909]{0:T(1024)}, u32[]{:S(2)}) copy-start(f32[6909]{0:T(1024)} %param.33) | copy-start | bytes 82912
  93.1 25.5 %copy-start.12 = (f32[6909]{0:T(1024)S(1)}, f32[6909]{0:T(1024)}, u32[]{:S(2)}) copy-start(f32[6909]{0:T(1024)} %param.32) | copy-start | bytes 82912
  93.1 25.5 %copy-start.13 = (f32[6909]{0:T(1024)S(1)}, f32[6909]{0:T(1024)}, u32[]{:S(2)}) copy-start(f32[6909]{0:T(1024)} %param.31) | copy-start | bytes 82912

commit v2 on v1

--- a/solution.py
+++ b/solution.py
@@ -158,6 +158,17 @@
 def main_kernel(
     n_pts,
     n_sub,
+    pts_hbm,
+    route_hbm,
+    labels_hbm,
+    src_hbm,
+    pool_hbm,
+    sample_hbm,
+    cnbr_hbm,
+    owner_hbm,
+    mats_hbm,
+    flat_ref,
+    out_ref,
     pts_ref,
     route_ref,
     labels_ref,
@@ -166,9 +177,7 @@
     sample_ref,
     cnbr_ref,
     owner_ref,
-    flat_ref,
     mats_ref,
-    out_ref,
     data,
     sacc,
     sendb,
@@ -223,6 +232,7 @@
     gat_recv,
     sib_send,
     sib_recv,
+    load_sem,
 ):
     fine = route_ref.shape[1]
     coarse = sample_ref.shape[1]
@@ -239,6 +249,15 @@
     sub = lax.axis_index("sub")
     half_at = pl.multiple_of(sub * half, half)
 
+    held = (pts_hbm, route_hbm, labels_hbm, src_hbm, mats_hbm, sample_hbm, pool_hbm, cnbr_hbm, owner_hbm)
+    near = (pts_ref, route_ref, labels_ref, src_ref, mats_ref, sample_ref, pool_ref, cnbr_ref, owner_ref)
+    loads = [
+        pltpu.make_async_copy(source, target, load_sem.at[number])
+        for number, (source, target) in enumerate(zip(held, near))
+    ]
+    for load in loads:
+        load.start()
+
     barrier = pltpu.get_barrier_semaphore()
 
     def greet(step, carry):
@@ -259,6 +278,8 @@
             device_id_type=MESH,
         )
 
+    for load in loads[0:5]:
+        load.wait()
     data[0:6, :] = pts_ref[...].astype(F32)
     data[6:8, :] = jnp.zeros((2, fine), F32)
     source_rows = src_ref[...]
@@ -317,7 +338,6 @@
         return carry
 
     lax.fori_loop(1, n_pts, send_blocks, 0)
-    lax.fori_loop(1, n_pts, send_mats, 0)
     recv[sub * n_pts + me] = sendb[me]
     matall[me] = matmine[...]
 
@@ -365,6 +385,9 @@
         return carry
 
     lax.fori_loop(1, n_pts, wait_blocks, 0)
+    lax.fori_loop(1, n_pts, send_mats, 0)
+    for load in loads[5:]:
+        load.wait()
     mine = recv.at[pl.ds(sub * n_pts, n_pts)]
     forward = sibling(0, mine, mine)
     forward.start()
@@ -412,14 +435,14 @@
         pin[k] = value
         return jnp.maximum(most, value)
 
-    most = lax.fori_loop(0, NEIGH, pool_step, jnp.full((C1, half), -jnp.inf, F32))
+    most = lax.fori_loop(0, NEIGH, pool_step, jnp.full((C1, half), -jnp.inf, F32), unroll=4)
 
     def exp_step(k, total):
         value = jnp.exp(pin[k] - most)
         pin[k] = value
         return total + value
 
-    total = lax.fori_loop(0, NEIGH, exp_step, jnp.zeros((C1, half), F32))
+    total = lax.fori_loop(0, NEIGH, exp_step, jnp.zeros((C1, half), F32), unroll=4)
     pooled = most + jnp.log(total)
     pooled_ref[...] = pooled
     rsum_ref[...] = 1.0 / total
@@ -490,21 +513,21 @@
         sc[k] = score
         return jnp.maximum(most, score)
 
-    top = lax.fori_loop(0, NEIGH, attend, jnp.full((GROUPS, half), -jnp.inf, F32))
+    top = lax.fori_loop(0, NEIGH, attend, jnp.full((GROUPS, half), -jnp.inf, F32), unroll=4)
 
     def weigh(k, total):
         value = jnp.exp(sc[k] - top)
         sc[k] = value
         return total + value
 
-    scale = 1.0 / lax.fori_loop(0, NEIGH, weigh, jnp.zeros((GROUPS, half), F32))
+    scale = 1.0 / lax.fori_loop(0, NEIGH, weigh, jnp.zeros((GROUPS, half), F32), unroll=8)
 
     def mix(k, total):
         weight = sc[k] * scale
         sc[k] = weight
         return total + expand(weight) * car[k]
 
-    mixed = lax.fori_loop(0, NEIGH, mix, jnp.zeros((C1, half), F32))
+    mixed = lax.fori_loop(0, NEIGH, mix, jnp.zeros((C1, half), F32), unroll=4)
     mixed_ref[...] = mixed
     block = pooled_ref[...] + dot(w_out_t, mixed.astype(BF16))
     blk_ref[...] = block
@@ -566,7 +589,7 @@
         dcp[...] += dot_nt(spread, jnp.concatenate(hots, 1)).reshape(parts, C0, LOW_B)
         return loss
 
-    loss = lax.fori_loop(0, slots // span, fine_step, jnp.zeros((1, span), F32))
+    loss = lax.fori_loop(0, slots // span, fine_step, jnp.zeros((1, span), F32), unroll=2)
 
     other = (1 - sub) * my_parts
     own = sub * my_parts
@@ -626,7 +649,7 @@
         dkp[...] += dot_nt(spread, ohs[k]).reshape(parts, C1 + 8, LOW_B)
         return total + ds1_kept
 
-    ds1_total = lax.fori_loop(0, NEIGH, attend_back, jnp.zeros((GROUPS, half), F32))
+    ds1_total = lax.fori_loop(0, NEIGH, attend_back, jnp.zeros((GROUPS, half), F32), unroll=4)
     give_dkv = sibling(4, dkp.at[pl.ds(other, my_parts)], dkr)
     give_dkv.start()
     give_dkv.wait_recv()
@@ -651,7 +674,7 @@
         gb[:, 0:96] += dot_nt(joined, jnp.concatenate([dpin, dstem], 0))
         return carry
 
-    lax.fori_loop(0, NEIGH, pool_back, 0)
+    lax.fori_loop(0, NEIGH, pool_back, 0, unroll=4)
 
     left = lanes_of(64, LANES) < 64
     gd_out = gd[64:128, :]
@@ -750,22 +773,37 @@
     out_ref[...] = gfull[...]
 
 
-def orthonormal_pair(matrix):
+def orthonormal_pair(matrix, width=8):
     size = matrix.shape[0]
-    lane = lanes_of(size, 2 * size)
-    left = lane < size
+    left = lanes_of(size, 2 * size) < size
     column = lanes_of(1, 2 * size)
     left_row = column < size
     place_row = jnp.where(left_row, column, column - size)
+
+    def spread(values, halves, at):
+        return jnp.where(halves, values[:, at : at + 1], values[:, size + at : size + at + 1])
+
     for repeat in range(2):
-        for j in range(size):
-            pivot = jnp.where(left, matrix[:, j : j + 1], matrix[:, size + j : size + j + 1])
-            products = jnp.sum(pivot * matrix, axis=0, keepdims=True)
-            norms = jnp.where(
-                left_row, products[:, j : j + 1], products[:, size + j : size + j + 1]
-            )
-            factor = jnp.where(place_row > j, products / norms, 0.0)
-            matrix = matrix - pivot * factor
+        for first in range(0, size, width):
+            span = range(width)
+            pivots = [spread(matrix, left, first + i) for i in span]
+            products = [jnp.sum(pivot * matrix, axis=0, keepdims=True) for pivot in pivots]
+            gram = [
+                [spread(products[i], left_row, first + l) if l >= i else None for l in span]
+                for i in span
+            ]
+            taken = 0.0
+            for i in span:
+                inverse = 1.0 / gram[i][i]
+                for l in range(i + 1, width):
+                    part = gram[i][l] * inverse
+                    pivots[l] = pivots[l] - part * pivots[i]
+                    products[l] = products[l] - part * products[i]
+                    for m in range(l, width):
+                        gram[l][m] = gram[l][m] - part * gram[i][m]
+                factor = jnp.where(place_row > first + i, products[i] * inverse, 0.0)
+                taken = taken + pivots[i] * factor
+            matrix = matrix - taken
         matrix = matrix * lax.rsqrt(jnp.sum(matrix * matrix, axis=0, keepdims=True))
     return matrix
 
@@ -905,6 +943,15 @@
     smem = pl.BlockSpec(memory_space=pltpu.SMEM)
     dma = pltpu.SemaphoreType.DMA
     scratch = [
+        VMEM((6, fine), BF16),
+        VMEM((1, fine), I32),
+        VMEM((1, fine), I32),
+        VMEM((3, fine), I32),
+        VMEM((NEIGH, coarse), I32),
+        VMEM((1, coarse), I32),
+        VMEM((NEIGH, coarse), I32),
+        pltpu.SMEM((NMATS,), I32),
+        VMEM((C1, C1), F32),
         VMEM((16, fine), F32),
         VMEM((n_pts * 16, cap), F32),
         VMEM((n_pts, 16, cap), BF16),
@@ -959,15 +1006,16 @@
         dma((n_pts,)),
         dma((8,)),
         dma((8,)),
+        dma((9,)),
     ]
     reduced = pl.pallas_call(
         functools.partial(main_kernel, n_pts, n_sub),
         out_shape=jax.ShapeDtypeStruct((256, LANES), F32),
-        in_specs=[vmem] * 7 + [smem] + [vmem] * 2,
+        in_specs=[pl.BlockSpec(memory_space=pltpu.HBM)] * 9 + [vmem],
         out_specs=vmem,
         scratch_shapes=scratch,
         compiler_params=pltpu.CompilerParams(
-            collective_id=0, has_side_effects=True, vmem_limit_bytes=48 * 1024 * 1024
+            collective_id=0, has_side_effects=True, vmem_limit_bytes=60 * 1024 * 1024
         ),
     )(
         points.T,
@@ -978,8 +1026,8 @@
         sample.reshape(1, coarse),
         coarse_nbr.T,
         owner,
+        mats[0],
         flat2,
-        mats[0],
     )
     square = jax.ShapeDtypeStruct((C1, C1), F32)
     results = pl.pallas_call(

time: 122 us -> 92.6 us (0.76)
  Pallas kernels: 111 us -> 86.5 us
  local copies, waits for them, and re-layouts: 7.29 us -> 2.73 us
    pallas_call x1, Pallas kernels: 25.4 us -> 9.32 us  [local(): pl.pallas_call(soap_kernel, out_shape=[square] * 8 + [jax.ShapeDtypeStruc...]
    pallas_call x1, Pallas kernels: 85.8 us -> 77.2 us  [local(): pl.pallas_call(functools.partial(main_kernel, n_pts, n_sub), out_shape=ja...]
    unnamed x28 -> x8, local copies, waits for them, and re-layouts: 5.19 us -> 0.03 us
where the time goes in v2:
time: 92.6 us; the launch traced here: 92.1 us
  Pallas kernels  86.5 us (93%)
  local copies, waits for them, and re-layouts  2.73 us (3%)
  between operations  1.46 us (2%)
  other arithmetic  1.4 us (2%)
    pallas_call x1, Pallas kernels, local(): pl.pallas_call(functools.partial(main_kernel, n_pts, n_sub), out_shape=ja...  77.2 us
    pallas_call x1, Pallas kernels, local(): pl.pallas_call(soap_kernel, out_shape=[square] * 8 + [jax.ShapeDtypeStruc...  9.32 us

profile of v2, /device:TPU:0, one launch (start us, length us, event | category | flops | bytes accessed | tf_op | source)
XLA Modules:
  0.0 92.1 jit_solution(12302979706609035732)
XLA Ops:
  0.6 1.4 %pad_bitcast_fusion.flat_ref = f32[64,128]{1,0:T(8,128)} fusion(f32[6909]{0:T(1024)} %param.30), kind=kLoop, calls=%fused_computation.1 | loop fusion | bytes 60404 | tf_op jit(solution)/shard_map/reshape | solution.py:941
  2.0 77.2 %shard_map.308.grads_ref = f32[256,128]{1,0:T(8,128)} custom-call(bf16[6,2048]{1,0:T(8,128)(2,1)} %bitcast.34, s32[1,2048]{1,0:T(1,128)} %bitcast.44, s32[1,2048]{1,0:T(1,128)} %bitcast.45, s32[3,2048]{1,0:T(4,128)} %bitcast.35, s32[16,1024]{1,0:T(8,128)} %bitcast.32, s32[1,1024]{1,0:T(1,128)} %bitcast.46, s32[16,1024]{1,0:T(8,128)} %bitcast.33, ...), custom_call_target="tpu_custom_call" | custom-call | tf_op jit(solution)/shard_map/pallas_call | solution.py:1011
  79.9 0.0 copy-start
  79.9 0.0 copy-start.1
  79.9 0.0 copy-start.2
  79.9 0.0 copy-start.3
  79.9 9.3 %shard_map.309 = (f32[64,64]{1,0:T(8,128)}, f32[64,64]{1,0:T(8,128)}, f32[64,64]{1,0:T(8,128)}, f32[64,64]{1,0:T(8,128)}, f32[64,64]{1,0:T(8,128)}, /*index=5*/f...) custom-call(f32[256,128]{1,0:T(8,128)} %shard_map.308.grads_ref, ...), custom_call_target="tpu_custom_call" | custom-call | tf_op jit(solution)/shard_map/pallas_call | solution.py:1033
  89.4 0.0 copy-done
  89.4 0.0 copy-done.1
  89.4 0.0 copy-done.2
  89.4 0.0 copy-done.3
  89.4 1.4 %multiply_add_fusion = (f32[6909]{0:T(1024)}, f32[6909]{0:T(1024)}, f32[6909]{0:T(1024)}, f32[6909]{0:T(1024)}) fusion(f32[6909]{0:T(1024)S(1)} %copy-done.1, f32[6909]{0:T(1024)S(1)} %copy-done, f32[]{:T(128)} %bitcast.20, f32[]{:T(128)} %bitcast.19, f32[7168]{0:T(1024)} %bitcast.43, f32[6909]{0:T(1024)S(1)} %copy-done.2, f32[6909]{0:T(1024)S(1)} %copy-done.3), kind=kLoop, calls=%fused_computation.3 | loop fusion | flops 124362 | bytes 248732 | tf_op jit(solution)/shard_map/add | solution.py:905
  90.8 1.3 %fusion.2 = (f32[1,1]{1,0:T(1,128)}, f32[1,1]{1,0:T(1,128)}) fusion(f32[8,128]{1,0:T(8,128)} %get-tuple-element.24), kind=kLoop, calls=%fused_computation.6 | loop fusion | bytes 16 | tf_op jit(solution)/shard_map/slice | solution.py:1058
Async XLA Ops:
  79.9 9.5 %copy-start = (f32[6909]{0:T(1024)S(1)}, f32[6909]{0:T(1024)}, u32[]{:S(2)}) copy-start(f32[6909]{0:T(1024)} %param.30) | copy-start | bytes 82912
  79.9 9.5 %copy-start.1 = (f32[6909]{0:T(1024)S(1)}, f32[6909]{0:T(1024)}, u32[]{:S(2)}) copy-start(f32[6909]{0:T(1024)} %param.33) | copy-start | bytes 82912
  79.9 9.5 %copy-start.2 = (f32[6909]{0:T(1024)S(1)}, f32[6909]{0:T(1024)}, u32[]{:S(2)}) copy-start(f32[6909]{0:T(1024)} %param.32) | copy-start | bytes 82912
  79.9 9.5 %copy-start.3 = (f32[6909]{0:T(1024)S(1)}, f32[6909]{0:T(1024)}, u32[]{:S(2)}) copy-start(f32[6909]{0:T(1024)} %param.31) | copy-start | bytes 82912

commit v3 on v2

--- a/solution.py
+++ b/solution.py
@@ -192,13 +192,21 @@
     rsum_ref,
     ctab,
     btab,
+    near,
     est,
+    gst,
     ohs,
     car,
     sc,
     mixed_ref,
     blk_ref,
     slot,
+    fin,
+    fgr,
+    skp,
+    foh,
+    fsrc,
+    fwt,
     dcp,
     dcr,
     dkp,
@@ -239,6 +247,7 @@
     cap = sendb.shape[2]
     slots = n_pts * cap
     half = coarse // n_sub
+    edges = NEIGH * half
     sources = n_sub * n_pts
     parts = coarse // LOW_B
     my_parts = parts // n_sub
@@ -249,11 +258,11 @@
     sub = lax.axis_index("sub")
     half_at = pl.multiple_of(sub * half, half)
 
-    held = (pts_hbm, route_hbm, labels_hbm, src_hbm, mats_hbm, sample_hbm, pool_hbm, cnbr_hbm, owner_hbm)
-    near = (pts_ref, route_ref, labels_ref, src_ref, mats_ref, sample_ref, pool_ref, cnbr_ref, owner_ref)
+    far_refs = (pts_hbm, route_hbm, labels_hbm, src_hbm, mats_hbm, sample_hbm, pool_hbm, cnbr_hbm, owner_hbm)
+    near_refs = (pts_ref, route_ref, labels_ref, src_ref, mats_ref, sample_ref, pool_ref, cnbr_ref, owner_ref)
     loads = [
         pltpu.make_async_copy(source, target, load_sem.at[number])
-        for number, (source, target) in enumerate(zip(held, near))
+        for number, (source, target) in enumerate(zip(far_refs, near_refs))
     ]
     for load in loads:
         load.start()
@@ -408,11 +417,14 @@
         keepdims=True,
     )
     total_fine = float(fine * n_pts * n_sub)
-    class_w = jnp.where(rows_of(16, 1) < NCLS, total_fine / (NCLS * class_counts), 0.0)
+    class_w = jnp.where(
+        rows_of(16, 1) < NCLS, total_fine / (NCLS * class_counts) * (1.0 / total_fine), 0.0
+    )
 
     def gather_points(index):
         hot = onehot(index & (cap - 1), cap)
-        return pick(dot(tabb[...], hot), lax.shift_right_logical(index, shift), sources)
+        high = jnp.broadcast_to(lax.shift_right_logical(index, shift), (8, index.shape[1]))
+        return pick(dot(tabb[...], hot), high, sources)
 
     zeros8 = jnp.zeros((8, span), F32)
     for chunk in range(coarse // span):
@@ -422,30 +434,55 @@
     centre = cen[:, pl.ds(half_at, half)]
     centre_low = jnp.concatenate([centre, zeros8], 0).astype(BF16)
     w_xyz_t = jnp.where(lanes_of(C1, 16) < 3, wd[...].T[0:C1, 0:16], 0.0).astype(BF16)
-    centre_term = dot(w_xyz_t, centre_low)
-
-    def pool_step(k, most):
+    pool_base = b_down - dot(w_xyz_t, centre_low)
+
+    def at_edge(k):
+        return pl.ds(pl.multiple_of(k * half, half), half)
+
+    def every_edge(step, unroll):
+        def run(k, carry):
+            step(k, at_edge(k))
+            return carry
+
+        lax.fori_loop(0, NEIGH, run, 0, unroll=unroll)
+
+    def pool_gather(k, lanes):
         found = gather_points(pool_ref[pl.ds(k, 1), pl.ds(half_at, half)])
-        low = jnp.concatenate([found, zeros8], 0).astype(BF16)
-        stem = relu(dot(w_stem_t, low) + b_stem)
-        joined = jnp.concatenate([found, zeros8, stem], 0).astype(BF16)
-        cat[k] = joined
-        projected = dot(w_down_t, joined).astype(BF16).astype(F32)
-        value = projected - centre_term + b_down
-        pin[k] = value
-        return jnp.maximum(most, value)
-
-    most = lax.fori_loop(0, NEIGH, pool_step, jnp.full((C1, half), -jnp.inf, F32), unroll=4)
-
-    def exp_step(k, total):
-        value = jnp.exp(pin[k] - most)
-        pin[k] = value
-        return total + value
-
-    total = lax.fori_loop(0, NEIGH, exp_step, jnp.zeros((C1, half), F32), unroll=4)
-    pooled = most + jnp.log(total)
-    pooled_ref[...] = pooled
-    rsum_ref[...] = 1.0 / total
+        cat[0:16, lanes] = jnp.concatenate([found, zeros8], 0).astype(BF16)
+
+    def pool_stem(k, lanes):
+        cat[16:48, lanes] = relu(dot(w_stem_t, cat[0:16, lanes]) + b_stem).astype(BF16)
+
+    def pool_project(k, lanes):
+        pin[:, lanes] = dot(w_down_t, cat[:, lanes]).astype(BF16).astype(F32) + pool_base
+
+    every_edge(pool_gather, 4)
+    every_edge(pool_stem, 16)
+    every_edge(pool_project, 16)
+
+    def tree(combine, values):
+        while len(values) > 1:
+            paired = [combine(values[i], values[i + 1]) for i in range(0, len(values) - 1, 2)]
+            values = paired + ([values[-1]] if len(values) % 2 else [])
+        return values[0]
+
+    wide = 256
+
+    def log_sum(r, carry):
+        rows = pl.ds(pl.multiple_of(r * 8, 8), 8)
+        for start in range(0, half, wide):
+            spots = [slice(k * half + start, k * half + start + wide) for k in range(NEIGH)]
+            values = [pin[rows, spot] for spot in spots]
+            most = tree(jnp.maximum, values)
+            values = [jnp.exp(value - most) for value in values]
+            for spot, value in zip(spots, values):
+                pin[rows, spot] = value
+            total = tree(jnp.add, values)
+            pooled_ref[rows, start : start + wide] = most + jnp.log(total)
+            rsum_ref[rows, start : start + wide] = 1.0 / total
+        return carry
+
+    lax.fori_loop(0, C1 // 8, log_sum, 0, unroll=2)
 
     def table_rows(values, target):
         for part in range(my_parts):
@@ -455,7 +492,7 @@
             )
             target[sub * my_parts + part] = stacked.astype(BF16)
 
-    table_rows(pooled, ctab)
+    table_rows(pooled_ref[...], ctab)
     my_ctab = ctab.at[pl.ds(sub * my_parts, my_parts)]
     give_pooled = sibling(1, my_ctab, my_ctab)
     give_pooled.start()
@@ -471,130 +508,179 @@
         folded = matall[owner_ref[position]].astype(F32)
         return jnp.concatenate([folded[:, 0:C1], folded[:, C1 : 2 * C1]], 0)
 
-    w_qkv32 = jnp.concatenate([layer(0), layer(1), layer(2)], 1)
-    w_qkv = w_qkv32.astype(BF16)
-    w_query_t = w_qkv32[:, 0:C1].T.astype(BF16)
-    w_kv_t = jnp.concatenate([w_qkv32[:, C1 : 2 * C1].T, w_qkv32[:, 2 * C1 :].T], 0).astype(BF16)
-    w_pos2_32 = layer(3)
+    w_query, w_key, w_value, w_pos2_32, w_out_32 = [layer(position) for position in range(NMATS)]
+    w_qkv = jnp.concatenate([w_query, w_key, w_value], 1).astype(BF16)
+    w_query_t = w_query.T.astype(BF16)
     w_pos2 = w_pos2_32.astype(BF16)
-    w_pos2_t = w_pos2_32.T.astype(BF16)
-    w_out_32 = layer(4)
+    w_pos2_t = w_pos2_32.T
+    w_edge_t = jnp.concatenate(
+        [
+            jnp.concatenate([-w_key.T, w_pos2_t], 1),
+            jnp.concatenate([w_value.T, w_pos2_t], 1),
+        ],
+        0,
+    ).astype(BF16)
     w_out = w_out_32.astype(BF16)
     w_out_t = w_out_32.T.astype(BF16)
-    pooled_low = pooled.astype(BF16)
-    queries = dot(w_query_t, pooled_low)
+    queries = dot(w_query_t, pooled_ref[...].astype(BF16))
+
+    def at_slot(step):
+        return pl.ds(pl.multiple_of(step * span, span), span)
+
+    def every_slot(step, unroll):
+        def run(j, carry):
+            step(j, at_slot(j))
+            return carry
+
+        lax.fori_loop(0, slots // span, run, 0, unroll=unroll)
+
+    def fine_points(j, lanes):
+        ones = jnp.where(rows_of(8, span) == 7, 1.0, slot[0:8, lanes])
+        fin[0:16, lanes] = jnp.concatenate([ones, zeros8], 0).astype(BF16)
+
+    def fine_stem(j, lanes):
+        fin[16:48, lanes] = relu(dot(w_stem_t, fin[0:16, lanes]) + b_stem).astype(BF16)
+
+    def fine_skip(j, lanes):
+        skp[:, lanes] = dot(w_skip_t, fin[16:48, lanes])
+
+    every_slot(fine_points, 4)
+    every_slot(fine_stem, 8)
+    every_slot(fine_skip, 8)
     give_pooled.wait_recv()
 
-    def expand(values):
-        return jnp.concatenate(
-            [jnp.broadcast_to(values[g : g + 1], (8, values.shape[1])) for g in range(GROUPS)], 0
-        )
-
-    def attend(k, most):
+    def attend_gather(k, lanes):
         index = cnbr_ref[pl.ds(k, 1), pl.ds(half_at, half)]
+        hot = onehot(index & (LOW_B - 1), LOW_B)
+        ohs[:, lanes] = hot
         high = lax.shift_right_logical(index, low_shift)
-        hot = onehot(index & (LOW_B - 1), LOW_B)
-        ohs[k] = hot
         found = pick(dot(ctab[...].reshape(parts * CH, LOW_B), hot), high, parts)
-        near = found[0:C1].astype(BF16)
-        rows = dot(w_kv_t, near)
+        near[:, lanes] = found[0:C1].astype(BF16)
         offset = jnp.where(rows_of(8, half) == 7, 1.0, centre - found[C1 : C1 + 8])
-        off_low = jnp.concatenate([zeros8, offset], 0).astype(BF16)
-        pos_low = relu(dot(w_pos_t, off_low) + b_pos).astype(BF16)
-        pos_enc = dot(w_pos2_t, pos_low)
-        edge_low = (queries - rows[0:C1] + pos_enc).astype(BF16)
-        act = relu(dot(w_att1_t, edge_low) + b_att1)
-        act_off = jnp.concatenate([act, offset], 0).astype(BF16)
-        score = dot(w_att2_t, act_off) + b_att2
-        est[k, 0:64, :] = edge_low
-        est[k, 64:128, :] = pos_low
-        est[k, 128:144, :] = act_off
-        car[k] = rows[C1 : 2 * C1] + pos_enc
-        sc[k] = score
-        return jnp.maximum(most, score)
-
-    top = lax.fori_loop(0, NEIGH, attend, jnp.full((GROUPS, half), -jnp.inf, F32), unroll=4)
-
-    def weigh(k, total):
-        value = jnp.exp(sc[k] - top)
-        sc[k] = value
-        return total + value
-
-    scale = 1.0 / lax.fori_loop(0, NEIGH, weigh, jnp.zeros((GROUPS, half), F32), unroll=8)
-
-    def mix(k, total):
-        weight = sc[k] * scale
-        sc[k] = weight
-        return total + expand(weight) * car[k]
-
-    mixed = lax.fori_loop(0, NEIGH, mix, jnp.zeros((C1, half), F32), unroll=4)
-    mixed_ref[...] = mixed
-    block = pooled_ref[...] + dot(w_out_t, mixed.astype(BF16))
+        est[128:144, lanes] = jnp.concatenate([zeros8, offset], 0).astype(BF16)
+
+    def attend_pos(k, lanes):
+        est[64:128, lanes] = relu(dot(w_pos_t, est[128:144, lanes]) + b_pos).astype(BF16)
+
+    def attend_edge(k, lanes):
+        both = dot(w_edge_t, jnp.concatenate([near[:, lanes], est[64:128, lanes]], 0))
+        est[0:64, lanes] = (queries + both[0:C1]).astype(BF16)
+        car[:, lanes] = both[C1 : 2 * C1]
+
+    def attend_act(k, lanes):
+        act = relu(dot(w_att1_t, est[0:64, lanes]) + b_att1)
+        offset = est[128:144, lanes].astype(F32)[8:16]
+        est[128:144, lanes] = jnp.concatenate([act, offset], 0).astype(BF16)
+
+    def attend_score(k, lanes):
+        sc[:, lanes] = dot(w_att2_t, est[128:144, lanes]) + b_att2
+
+    every_edge(attend_gather, 4)
+    every_edge(attend_pos, 16)
+    every_edge(attend_edge, 16)
+    every_edge(attend_act, 16)
+    every_edge(attend_score, 16)
+
+    for start in range(0, half, wide):
+        spots = [slice(k * half + start, k * half + start + wide) for k in range(NEIGH)]
+        values = [sc[:, spot] for spot in spots]
+        most = tree(jnp.maximum, values)
+        values = [jnp.exp(value - most) for value in values]
+        scale = 1.0 / tree(jnp.add, values)
+        for spot, value in zip(spots, values):
+            sc[:, spot] = value * scale
+
+    for g in range(GROUPS):
+        rows = slice(8 * g, 8 * g + 8)
+        for start in range(0, half, wide):
+            spots = [slice(k * half + start, k * half + start + wide) for k in range(NEIGH)]
+            terms = [
+                jnp.broadcast_to(sc[g : g + 1, spot], (8, wide)) * car[rows, spot]
+                for spot in spots
+            ]
+            mixed_ref[rows, start : start + wide] = tree(jnp.add, terms)
+
+    block = pooled_ref[...] + dot(w_out_t, mixed_ref[...].astype(BF16))
     blk_ref[...] = block
     table_rows(block, btab)
     my_btab = btab.at[pl.ds(sub * my_parts, my_parts)]
     give_block = sibling(2, my_btab, my_btab)
     give_block.start()
+
+    def source_of(lanes, i):
+        index = (32.0 * slot[8 + i : 9 + i, lanes] + slot[11 + i : 12 + i, lanes]).astype(I32)
+        return index & (LOW_B - 1), lax.shift_right_logical(index, low_shift)
+
+    def fine_hot(j, lanes):
+        for i in range(3):
+            foh[i, :, lanes] = onehot(source_of(lanes, i)[0], LOW_B)
+
+    every_slot(fine_hot, 2)
     give_block.wait_recv()
 
-    ga[...] = jnp.zeros_like(ga)
-    dcp[...] = jnp.zeros_like(dcp)
-
-    def fine_step(step, loss):
-        at = pl.multiple_of(step * span, span)
-        rows = slot[:, pl.ds(at, span)]
-        points = rows[0:8]
-        source = (32.0 * rows[8:11] + rows[11:14]).astype(I32)
-        label = rows[14:15].astype(I32)
-        hots = []
-        highs = []
-        ups = []
+    def fine_gather(j, lanes):
+        points = slot[0:8, lanes]
         inverses = []
         for i in range(3):
-            index = source[i : i + 1]
-            high = lax.shift_right_logical(index, low_shift)
-            hot = onehot(index & (LOW_B - 1), LOW_B)
-            found = pick(dot(btab[...].reshape(parts * CH, LOW_B), hot), high, parts)
-            ups.append(dot(w_up_t, found[0:C1].astype(BF16)) + b_up)
+            high = source_of(lanes, i)[1]
+            found = pick(dot(btab[...].reshape(parts * CH, LOW_B), foh[i, :, lanes]), high, parts)
+            fsrc[i, :, lanes] = found[0:C1].astype(BF16)
             diff = jnp.where(rows_of(8, span) < 3, points - found[C1 : C1 + 8], 0.0)
             inverses.append(1.0 / (jnp.sum(diff * diff, axis=0, keepdims=True) + INTERP_EPS))
-            hots.append(hot)
-            highs.append(high)
-        norm = inverses[0] + inverses[1] + inverses[2]
-        weights = [inverse / norm for inverse in inverses]
-        interp = weights[0] * ups[0] + weights[1] * ups[1] + weights[2] * ups[2]
-        interp = interp.astype(BF16).astype(F32)
-        ones = jnp.where(rows_of(8, span) == 7, 1.0, points)
-        points_low = jnp.concatenate([ones, zeros8], 0).astype(BF16)
-        stem_pre = dot(w_stem_t, points_low) + b_stem
-        stem_low = relu(stem_pre).astype(BF16)
-        joined = interp + dot(w_skip_t, stem_low)
-        joined_low = relu(joined).astype(BF16)
-        logits = dot(w_head_t, joined_low) + b_head
+        norm = 1.0 / (inverses[0] + inverses[1] + inverses[2])
+        for i in range(3):
+            fwt[i : i + 1, lanes] = inverses[i] * norm
+
+    def fine_join(j, lanes):
+        terms = [fwt[i : i + 1, lanes] * dot(w_up_t, fsrc[i, :, lanes]) for i in range(3)]
+        interp = (terms[0] + terms[1] + terms[2] + b_up).astype(BF16).astype(F32)
+        fin[48:80, lanes] = relu(interp + skp[:, lanes]).astype(BF16)
+
+    def fine_loss(j, loss):
+        lanes = at_slot(j)
+        logits = dot(w_head_t, fin[48:80, lanes]) + b_head
+        label = slot[14:15, lanes].astype(I32)
         hit = jnp.where(rows_of(16, span) + 1 == label, 1.0, 0.0)
-        row_w = jnp.sum(hit * class_w, axis=0, keepdims=True) * (1.0 / total_fine)
+        row_w = jnp.sum(hit * class_w, axis=0, keepdims=True)
         peak = jnp.max(logits, axis=0, keepdims=True)
-        lse = peak + jnp.log(jnp.sum(jnp.exp(logits - peak), axis=0, keepdims=True))
-        loss = loss + row_w * (lse - jnp.sum(hit * logits, axis=0, keepdims=True))
-        dlog_low = (row_w * (jnp.exp(logits - lse) - hit)).astype(BF16)
-        dfused_low = jnp.where(joined > 0, dot(w_head, dlog_low), 0.0).astype(BF16)
-        dfused = dfused_low.astype(F32)
-        dstem = jnp.where(stem_pre > 0, dot(w_skip, dfused_low), 0.0).astype(BF16)
-        inputs = jnp.concatenate([points_low, stem_low, joined_low], 0)
-        grads = jnp.concatenate([dfused_low, dstem, dlog_low], 0)
-        ga[:, 0:80] += dot_nt(inputs, grads)
-        spread = jnp.concatenate(
-            [place(weights[i] * dfused, highs[i], parts) for i in range(3)], 1
-        )
-        dcp[...] += dot_nt(spread, jnp.concatenate(hots, 1)).reshape(parts, C0, LOW_B)
-        return loss
-
-    loss = lax.fori_loop(0, slots // span, fine_step, jnp.zeros((1, span), F32), unroll=2)
+        raised = jnp.exp(logits - peak)
+        total = jnp.sum(raised, axis=0, keepdims=True)
+        named = jnp.sum(hit * logits, axis=0, keepdims=True)
+        fgr[64:80, lanes] = (row_w * (raised * (1.0 / total) - hit)).astype(BF16)
+        return loss + row_w * (peak + jnp.log(total) - named)
+
+    def fine_fused(j, lanes):
+        kept = fin[48:80, lanes].astype(F32) > 0
+        fgr[0:32, lanes] = jnp.where(kept, dot(w_head, fgr[64:80, lanes]), 0.0).astype(BF16)
+
+    def fine_scatter(j, lanes):
+        dfused = fgr[0:32, lanes].astype(F32)
+        total = 0.0
+        for i in range(3):
+            spread = place(fwt[i : i + 1, lanes] * dfused, source_of(lanes, i)[1], parts)
+            total = total + dot_nt(spread, foh[i, :, lanes])
+        dcp[...] += total.reshape(parts, C0, LOW_B)
+
+    def fine_back(j, lanes):
+        kept = fin[16:48, lanes].astype(F32) > 0
+        fgr[32:64, lanes] = jnp.where(kept, dot(w_skip, fgr[0:32, lanes]), 0.0).astype(BF16)
+
+    every_slot(fine_gather, 8)
+    every_slot(fine_join, 8)
+    loss = lax.fori_loop(0, slots // span, fine_loss, jnp.zeros((1, span), F32), unroll=4)
+    every_slot(fine_fused, 8)
+    dcp[...] = jnp.zeros_like(dcp)
+    every_slot(fine_scatter, 2)
 
     other = (1 - sub) * my_parts
     own = sub * my_parts
     give_dup = sibling(3, dcp.at[pl.ds(other, my_parts)], dcr)
     give_dup.start()
+    every_slot(fine_back, 8)
+    ga[...] = jnp.zeros_like(ga)
+    for start in range(0, slots, 4 * span):
+        lanes = slice(start, start + 4 * span)
+        ga[:, 0:80] += dot_nt(fin[:, lanes], fgr[:, lanes])
     give_dup.wait_recv()
 
     def own_half(partial, received):
@@ -606,11 +692,6 @@
     dblock = dot(w_up, dup_low)
     dbranch_low = dblock.astype(BF16)
     dmixed = dot(w_out, dbranch_low)
-    inputs = jnp.concatenate(
-        [blk_ref[...].astype(BF16), mixed_ref[...].astype(BF16), jnp.ones((16, half), BF16)], 0
-    )
-    grads = jnp.concatenate([dup_low, jnp.zeros((C0, half), BF16), dbranch_low], 0)
-    gd[...] = dot_nt(inputs, grads)
 
     def group_sum(values):
         return jnp.concatenate(
@@ -621,41 +702,64 @@
             0,
         )
 
+    def expand(values):
+        return jnp.concatenate(
+            [jnp.broadcast_to(values[g : g + 1], (8, values.shape[1])) for g in range(GROUPS)], 0
+        )
+
     centred = group_sum(dmixed * mixed_ref[...])
+
+    def back_score(k, lanes):
+        ds2 = sc[:, lanes] * (group_sum(dmixed * car[:, lanes]) - centred)
+        gst[128:144, lanes] = jnp.concatenate([ds2, zeros8], 0).astype(BF16)
+
+    def back_act(k, lanes):
+        scores = gst[128:144, lanes]
+        kept = est[128:144, lanes].astype(F32)[0:8] > 0
+        ds1 = jnp.where(kept, dot(w_att2, scores), 0.0)
+        ds2 = scores.astype(F32)[0:8]
+        gst[128:144, lanes] = jnp.concatenate([ds1, ds2], 0).astype(BF16)
+
+    def back_edge(k, lanes):
+        small = gst[128:144, lanes]
+        dcarried = expand(sc[:, lanes]) * dmixed
+        gst[64:128, lanes] = (dot(w_att1, small) + dcarried).astype(BF16)
+        index = cnbr_ref[pl.ds(k, 1), pl.ds(half_at, half)]
+        high = lax.shift_right_logical(index, low_shift)
+        spread = place(jnp.concatenate([dcarried, small.astype(F32)[0:8]], 0), high, parts)
+        dkp[...] += dot_nt(spread, ohs[:, lanes]).reshape(parts, C1 + 8, LOW_B)
+
+    def back_pos(k, lanes):
+        kept = est[64:128, lanes].astype(F32) > 0
+        gst[0:64, lanes] = jnp.where(kept, dot(w_pos2, gst[64:128, lanes]), 0.0).astype(BF16)
+
+    every_edge(back_score, 16)
+    every_edge(back_act, 16)
+    dkp[...] = jnp.zeros_like(dkp)
+    every_edge(back_edge, 16)
+    give_dkv = sibling(4, dkp.at[pl.ds(other, my_parts)], dkr)
+    give_dkv.start()
+    every_edge(back_pos, 16)
+    inputs = jnp.concatenate(
+        [blk_ref[...].astype(BF16), mixed_ref[...].astype(BF16), jnp.ones((16, half), BF16)], 0
+    )
+    grads = jnp.concatenate([dup_low, jnp.zeros((C0, half), BF16), dbranch_low], 0)
+    gd[...] = dot_nt(inputs, grads)
     gc[...] = jnp.zeros_like(gc)
     ge[...] = jnp.zeros_like(ge)
-    dkp[...] = jnp.zeros_like(dkp)
-
-    def attend_back(k, total):
-        weight = sc[k]
-        act_off = est[k, 128:144, :].astype(F32)
-        pos_low = est[k, 64:128, :]
-        ds2 = weight * (group_sum(dmixed * car[k]) - centred)
-        ds2_low = jnp.concatenate([ds2, zeros8], 0).astype(BF16)
-        ds1 = jnp.where(act_off[0:8] > 0, dot(w_att2, ds2_low), 0.0)
-        ds1_low = jnp.concatenate([ds1, zeros8], 0).astype(BF16)
-        ds1_kept = ds1_low.astype(F32)[0:8]
-        dedge = dot(w_att1, ds1_low)
-        dcarried = expand(weight) * dmixed
-        dpos_low = (dedge + dcarried).astype(BF16)
-        dpos_pre = jnp.where(pos_low.astype(F32) > 0, dot(w_pos2, dpos_low), 0.0).astype(BF16)
-        small = jnp.concatenate([ds1, ds2], 0).astype(BF16)
-        result = dot_nt(est[k], jnp.concatenate([dpos_pre, dpos_low, small], 0))
+    for start in range(0, edges, 4 * span):
+        lanes = slice(start, start + 4 * span)
+        result = dot_nt(est[:, lanes], gst[:, lanes])
         gc[...] += result[:, 0:128]
         ge[:, 0:16] += result[:, 128:144]
-        index = cnbr_ref[pl.ds(k, 1), pl.ds(half_at, half)]
-        high = lax.shift_right_logical(index, low_shift)
-        spread = place(jnp.concatenate([dcarried, ds1_kept], 0), high, parts)
-        dkp[...] += dot_nt(spread, ohs[k]).reshape(parts, C1 + 8, LOW_B)
-        return total + ds1_kept
-
-    ds1_total = lax.fori_loop(0, NEIGH, attend_back, jnp.zeros((GROUPS, half), F32), unroll=4)
-    give_dkv = sibling(4, dkp.at[pl.ds(other, my_parts)], dkr)
-    give_dkv.start()
+    ds1_total = tree(
+        jnp.add,
+        [gst[128:144, k * half : (k + 1) * half].astype(F32)[0:8] for k in range(NEIGH)],
+    )
+    w_att1_exact = w1[0:C1, 0:16].astype(BF16).astype(F32)[:, 0:8]
+    dqueries = exact(w_att1_exact, ds1_total)
     give_dkv.wait_recv()
     dkv = own_half(dkp, dkr)
-    w_att1_exact = w1[0:C1, 0:16].astype(BF16).astype(F32)[:, 0:8]
-    dqueries = exact(w_att1_exact, ds1_total)
     dkeys = -exact(w_att1_exact, dkv[C1 : C1 + 8])
     dqkv_low = jnp.concatenate([dqueries, dkeys, dkv[0:C1]], 0).astype(BF16)
     gbuf[...] = jnp.zeros_like(gbuf)
@@ -667,14 +771,16 @@
     gb[0:16, 0:C1] = dot_nt(centre_low, (-dpooled).astype(BF16))
     dscaled = dpooled * rsum_ref[...]
 
-    def pool_back(k, carry):
-        dpin = (pin[k] * dscaled).astype(BF16)
-        joined = cat[k]
-        dstem = jnp.where(joined[16:48].astype(F32) > 0, dot(w_down_stem, dpin), 0.0).astype(BF16)
-        gb[:, 0:96] += dot_nt(joined, jnp.concatenate([dpin, dstem], 0))
-        return carry
-
-    lax.fori_loop(0, NEIGH, pool_back, 0, unroll=4)
+    def pool_back(k, lanes):
+        dpin = (pin[:, lanes] * dscaled).astype(BF16)
+        gst[0:64, lanes] = dpin
+        kept = cat[16:48, lanes].astype(F32) > 0
+        gst[64:96, lanes] = jnp.where(kept, dot(w_down_stem, dpin), 0.0).astype(BF16)
+
+    every_edge(pool_back, 16)
+    for start in range(0, edges, 4 * span):
+        lanes = slice(start, start + 4 * span)
+        gb[:, 0:96] += dot_nt(cat[:, lanes], gst[0:96, lanes])
 
     left = lanes_of(64, LANES) < 64
     gd_out = gd[64:128, :]
@@ -936,6 +1042,7 @@
     slots = n_pts * cap
     sources = n_sub * n_pts
     half = coarse // n_sub
+    edges = NEIGH * half
     parts = coarse // LOW_B
     my_parts = parts // n_sub
     flat2 = jnp.pad(flat, (0, FLAT_ROWS * LANES - FLAT)).reshape(FLAT_ROWS, LANES)
@@ -960,19 +1067,27 @@
         VMEM((n_pts, 32, LANES), BF16),
         VMEM((sources * 8, cap), BF16),
         VMEM((8, coarse), F32),
-        VMEM((NEIGH, C1, half), F32),
-        VMEM((NEIGH, 48, half), BF16),
+        VMEM((C1, edges), F32),
+        VMEM((48, edges), BF16),
         VMEM((C1, half), F32),
         VMEM((C1, half), F32),
         VMEM((parts, CH, LOW_B), BF16),
         VMEM((parts, CH, LOW_B), BF16),
-        VMEM((NEIGH, 144, half), BF16),
-        VMEM((NEIGH, LOW_B, half), BF16),
-        VMEM((NEIGH, C1, half), F32),
-        VMEM((NEIGH, GROUPS, half), F32),
+        VMEM((C1, edges), BF16),
+        VMEM((144, edges), BF16),
+        VMEM((144, edges), BF16),
+        VMEM((LOW_B, edges), BF16),
+        VMEM((C1, edges), F32),
+        VMEM((GROUPS, edges), F32),
         VMEM((C1, half), F32),
         VMEM((C1, half), F32),
         VMEM((16, slots), F32),
+        VMEM((80, slots), BF16),
+        VMEM((80, slots), BF16),
+        VMEM((C0, slots), F32),
+        VMEM((3, LOW_B, slots), BF16),
+        VMEM((3, C1, slots), BF16),
+        VMEM((8, slots), F32),
         VMEM((parts, C0, LOW_B), F32),
         VMEM((my_parts, C0, LOW_B), F32),
         VMEM((parts, C1 + 8, LOW_B), F32),

time: 92.6 us -> 66.9 us (0.72)
  Pallas kernels: 86.5 us -> 60.9 us
    pallas_call x1, Pallas kernels: 77.2 us -> 51.5 us  [local(): pl.pallas_call(functools.partial(main_kernel, n_pts, n_sub), out_shape=ja...]
where the time goes in v3:
time: 66.9 us; the launch traced here: 66.5 us
  Pallas kernels  60.9 us (91%)
  local copies, waits for them, and re-layouts  2.73 us (4%)
  between operations  1.46 us (2%)
  other arithmetic  1.4 us (2%)
    pallas_call x1, Pallas kernels, local(): pl.pallas_call(functools.partial(main_kernel, n_pts, n_sub), out_shape=ja...  51.5 us
    pallas_call x1, Pallas kernels, local(): pl.pallas_call(soap_kernel, out_shape=[square] * 8 + [jax.ShapeDtypeStruc...  9.33 us
    add x1, other arithmetic, adam_update(): EMA_KEEP * average + (1.0 - EMA_KEEP) * weight_new  1.4 us
    reshape x1, local copies, waits for them, and re-layouts, local(): jnp.pad(flat, (0, FLAT_ROWS * LANES - FLAT)).reshape(FLAT_ROWS, LANES)  1.37 us
    slice x1, local copies, waits for them, and re-layouts, local(): results[9][0, 1]  1.34 us

profile of v3, /device:TPU:0, one launch (start us, length us, event | category | flops | bytes accessed | tf_op | source)
XLA Modules:
  0.0 66.5 jit_solution(2168806176629007489)
XLA Ops:
  0.6 1.4 %pad_bitcast_fusion.flat_ref = f32[64,128]{1,0:T(8,128)} fusion(f32[6909]{0:T(1024)} %param.30), kind=kLoop, calls=%fused_computation.1 | loop fusion | bytes 60404 | tf_op jit(solution)/shard_map/reshape | solution.py:1048
  2.0 51.5 %shard_map.308.grads_ref = f32[256,128]{1,0:T(8,128)} custom-call(bf16[6,2048]{1,0:T(8,128)(2,1)} %bitcast.34, s32[1,2048]{1,0:T(1,128)} %bitcast.44, s32[1,2048]{1,0:T(1,128)} %bitcast.45, s32[3,2048]{1,0:T(4,128)} %bitcast.35, s32[16,1024]{1,0:T(8,128)} %bitcast.32, s32[1,1024]{1,0:T(1,128)} %bitcast.46, s32[16,1024]{1,0:T(8,128)} %bitcast.33, ...), custom_call_target="tpu_custom_call" | custom-call | tf_op jit(solution)/shard_map/pallas_call | solution.py:1126
  54.2 0.0 copy-start
  54.2 0.0 copy-start.1
  54.2 0.0 copy-start.2
  54.2 0.0 copy-start.3
  54.3 9.3 %shard_map.309 = (f32[64,64]{1,0:T(8,128)}, f32[64,64]{1,0:T(8,128)}, f32[64,64]{1,0:T(8,128)}, f32[64,64]{1,0:T(8,128)}, f32[64,64]{1,0:T(8,128)}, /*index=5*/f...) custom-call(f32[256,128]{1,0:T(8,128)} %shard_map.308.grads_ref, ...), custom_call_target="tpu_custom_call" | custom-call | tf_op jit(solution)/shard_map/pallas_call | solution.py:1148
  63.7 0.0 copy-done
  63.7 0.0 copy-done.1
  63.7 0.0 copy-done.2
  63.7 0.0 copy-done.3
  63.7 1.4 %multiply_add_fusion = (f32[6909]{0:T(1024)}, f32[6909]{0:T(1024)}, f32[6909]{0:T(1024)}, f32[6909]{0:T(1024)}) fusion(f32[6909]{0:T(1024)S(1)} %copy-done.1, f32[6909]{0:T(1024)S(1)} %copy-done, f32[]{:T(128)} %bitcast.20, f32[]{:T(128)} %bitcast.19, f32[7168]{0:T(1024)} %bitcast.43, f32[6909]{0:T(1024)S(1)} %copy-done.2, f32[6909]{0:T(1024)S(1)} %copy-done.3), kind=kLoop, calls=%fused_computation.3 | loop fusion | flops 124362 | bytes 248732 | tf_op jit(solution)/shard_map/add | solution.py:1011
  65.1 1.3 %fusion.2 = (f32[1,1]{1,0:T(1,128)}, f32[1,1]{1,0:T(1,128)}) fusion(f32[8,128]{1,0:T(8,128)} %get-tuple-element.24), kind=kLoop, calls=%fused_computation.6 | loop fusion | bytes 16 | tf_op jit(solution)/shard_map/slice | solution.py:1173
Async XLA Ops:
  54.2 9.5 %copy-start = (f32[6909]{0:T(1024)S(1)}, f32[6909]{0:T(1024)}, u32[]{:S(2)}) copy-start(f32[6909]{0:T(1024)} %param.30) | copy-start | bytes 82912
  54.2 9.5 %copy-start.1 = (f32[6909]{0:T(1024)S(1)}, f32[6909]{0:T(1024)}, u32[]{:S(2)}) copy-start(f32[6909]{0:T(1024)} %param.33) | copy-start | bytes 82912
  54.2 9.5 %copy-start.2 = (f32[6909]{0:T(1024)S(1)}, f32[6909]{0:T(1024)}, u32[]{:S(2)}) copy-start(f32[6909]{0:T(1024)} %param.32) | copy-start | bytes 82912
  54.2 9.5 %copy-start.3 = (f32[6909]{0:T(1024)S(1)}, f32[6909]{0:T(1024)}, u32[]{:S(2)}) copy-start(f32[6909]{0:T(1024)} %param.31) | copy-start | bytes 82912

commit v4 on v3

--- a/solution.py
+++ b/solution.py
@@ -167,7 +167,7 @@
     cnbr_hbm,
     owner_hbm,
     mats_hbm,
-    flat_ref,
+    flat_hbm,
     out_ref,
     pts_ref,
     route_ref,
@@ -178,6 +178,8 @@
     cnbr_ref,
     owner_ref,
     mats_ref,
+    flat_line,
+    flat_ref,
     data,
     sacc,
     sendb,
@@ -264,13 +266,27 @@
         pltpu.make_async_copy(source, target, load_sem.at[number])
         for number, (source, target) in enumerate(zip(far_refs, near_refs))
     ]
+    loads.append(
+        pltpu.make_async_copy(flat_hbm, flat_line, load_sem.at[len(loads)])
+    )
     for load in loads:
         load.start()
 
     barrier = pltpu.get_barrier_semaphore()
 
+    powers = [2**k for k in range(n_pts.bit_length() - 1)]
+    my_bits = [lax.bitwise_and(lax.shift_right_logical(me, k), 1) for k in range(len(powers))]
+
+    def partner(step):
+        step = n_pts - step
+        found = 0
+        for k, power in enumerate(powers):
+            bit = lax.bitwise_and(my_bits[k] + lax.shift_right_logical(step, k), 1)
+            found = found + power * bit
+        return found
+
     def greet(step, carry):
-        peer = lax.rem(me + step, n_pts)
+        peer = partner(step)
         pl.semaphore_signal(barrier, inc=1, device_id={"pts": peer}, device_id_type=MESH)
         return carry
 
@@ -287,7 +303,7 @@
             device_id_type=MESH,
         )
 
-    for load in loads[0:5]:
+    for load in loads[0:5] + loads[9:]:
         load.wait()
     data[0:6, :] = pts_ref[...].astype(F32)
     data[6:8, :] = jnp.zeros((2, fine), F32)
@@ -339,11 +355,11 @@
         )
 
     def send_blocks(step, carry):
-        block_copy(lax.rem(me + step, n_pts), me).start()
+        block_copy(partner(step), me).start()
         return carry
 
     def send_mats(step, carry):
-        mat_copy(lax.rem(me + step, n_pts), me).start()
+        mat_copy(partner(step), me).start()
         return carry
 
     lax.fori_loop(1, n_pts, send_blocks, 0)
@@ -352,6 +368,8 @@
 
     for ref in (wst, wd, wp, w1, w2, wu, wsk, wh, bias):
         ref[...] = jnp.zeros_like(ref)
+    padded = jnp.pad(flat_line[...], (0, FLAT_ROWS * LANES - FLAT))
+    flat_ref[...] = padded.reshape(FLAT_ROWS, LANES)
     unpack(flat_ref, wst, OFF["w_stem"], 6, C0, 0)
     unpack(flat_ref, wd, OFF["w_down"], 3, C1, 0)
     unpack(flat_ref, wd, OFF["w_down"] + 3 * C1, C0, C1, 16)
@@ -389,13 +407,13 @@
     w_head = wh[0:C0, 0:16].astype(BF16)
 
     def wait_blocks(step, carry):
-        peer = lax.rem(me + step, n_pts)
+        peer = partner(step)
         block_copy(peer, peer).wait_recv()
         return carry
 
     lax.fori_loop(1, n_pts, wait_blocks, 0)
     lax.fori_loop(1, n_pts, send_mats, 0)
-    for load in loads[5:]:
+    for load in loads[5:9]:
         load.wait()
     mine = recv.at[pl.ds(sub * n_pts, n_pts)]
     forward = sibling(0, mine, mine)
@@ -498,7 +516,7 @@
     give_pooled.start()
 
     def wait_mats(step, carry):
-        peer = lax.rem(me + step, n_pts)
+        peer = partner(step)
         mat_copy(peer, peer).wait_recv()
         return carry
 
@@ -849,7 +867,7 @@
 
     def each_peer(run, limited):
         def body(step, carry):
-            peer = lax.rem(me + step, n_pts)
+            peer = partner(step)
             when(None if holds is None or not limited else peer < shards, lambda: run(peer))
             return carry
 
@@ -879,7 +897,11 @@
     out_ref[...] = gfull[...]
 
 
-def orthonormal_pair(matrix, width=8):
+def normalised(matrix):
+    return matrix * lax.rsqrt(jnp.sum(matrix * matrix, axis=0, keepdims=True))
+
+
+def gram_schmidt_pair(matrix, width=8):
     size = matrix.shape[0]
     left = lanes_of(size, 2 * size) < size
     column = lanes_of(1, 2 * size)
@@ -889,29 +911,78 @@
     def spread(values, halves, at):
         return jnp.where(halves, values[:, at : at + 1], values[:, size + at : size + at + 1])
 
+    for first in range(0, size, width):
+        span = range(width)
+        pivots = [spread(matrix, left, first + i) for i in span]
+        products = [jnp.sum(pivot * matrix, axis=0, keepdims=True) for pivot in pivots]
+        gram = [
+            [spread(products[i], left_row, first + l) if l >= i else None for l in span]
+            for i in span
+        ]
+        taken = 0.0
+        for i in span:
+            inverse = 1.0 / gram[i][i]
+            for l in range(i + 1, width):
+                part = gram[i][l] * inverse
+                pivots[l] = pivots[l] - part * pivots[i]
+                products[l] = products[l] - part * products[i]
+                for m in range(l, width):
+                    gram[l][m] = gram[l][m] - part * gram[i][m]
+            factor = jnp.where(place_row > first + i, products[i] * inverse, 0.0)
+            taken = taken + pivots[i] * factor
+        matrix = matrix - taken
+    return normalised(matrix)
+
+
+def careful_pair(matrix):
+    size = matrix.shape[0]
+    lane = lanes_of(size, 2 * size)
+    left = lane < size
+    place = jnp.where(left, lane, lane - size)
+
+    def column(j, matrix):
+        here = jnp.where(place == j, matrix, 0.0)
+        first = jnp.sum(jnp.where(left, here, 0.0), axis=1, keepdims=True)
+        second = jnp.sum(jnp.where(left, 0.0, here), axis=1, keepdims=True)
+        pivot = jnp.where(left, first, second)
+        pivot = pivot * lax.rsqrt(jnp.sum(pivot * pivot, axis=0, keepdims=True))
+        factor = jnp.sum(pivot * matrix, axis=0, keepdims=True)
+        return matrix - jnp.where(place > j, pivot * factor, 0.0)
+
     for repeat in range(2):
-        for first in range(0, size, width):
-            span = range(width)
-            pivots = [spread(matrix, left, first + i) for i in span]
-            products = [jnp.sum(pivot * matrix, axis=0, keepdims=True) for pivot in pivots]
-            gram = [
-                [spread(products[i], left_row, first + l) if l >= i else None for l in span]
-                for i in span
-            ]
-            taken = 0.0
-            for i in span:
-                inverse = 1.0 / gram[i][i]
-                for l in range(i + 1, width):
-                    part = gram[i][l] * inverse
-                    pivots[l] = pivots[l] - part * pivots[i]
-                    products[l] = products[l] - part * products[i]
-                    for m in range(l, width):
-                        gram[l][m] = gram[l][m] - part * gram[i][m]
-                factor = jnp.where(place_row > first + i, products[i] * inverse, 0.0)
-                taken = taken + pivots[i] * factor
-            matrix = matrix - taken
-        matrix = matrix * lax.rsqrt(jnp.sum(matrix * matrix, axis=0, keepdims=True))
+        matrix = normalised(lax.fori_loop(0, size, column, matrix))
     return matrix
+
+
+def departure(basis):
+    size = basis.shape[0]
+    same = rows_of(size, size) == lanes_of(size, size)
+    return exact(basis, basis, ((0,), (0,))) - jnp.where(same, 1.0, 0.0)
+
+
+def correct(basis, error):
+    size = basis.shape[0]
+    above = rows_of(size, size) < lanes_of(size, size)
+    same = rows_of(size, size) == lanes_of(size, size)
+    factor = jnp.where(above, error, jnp.where(same, 0.5 * error, 0.0))
+    return basis - exact(basis, factor)
+
+
+def orthonormal_pair(matrix, both_ref):
+    size = matrix.shape[0]
+    once = gram_schmidt_pair(matrix)
+    halves = [once[:, 0:size], once[:, size : 2 * size]]
+    errors = [departure(half) for half in halves]
+    worst = jnp.max(jnp.maximum(jnp.abs(errors[0]), jnp.abs(errors[1])))
+    halves = [correct(half, error) for half, error in zip(halves, errors)]
+    halves = [correct(half, departure(half)) for half in halves]
+    both_ref[...] = jnp.concatenate(halves, 1)
+
+    @pl.when(jnp.logical_not(worst < 0.01))
+    def _():
+        both_ref[...] = careful_pair(matrix)
+
+    return both_ref[...]
 
 
 def soap_kernel(
@@ -926,6 +997,10 @@
     basis_l_ref,
     basis_r_ref,
     average_ref,
+    flat_ref,
+    flat_mom_ref,
+    flat_sec_ref,
+    flat_ema_ref,
     weight_out,
     first_out,
     second_out,
@@ -935,21 +1010,42 @@
     basis_r_out,
     average_out,
     flat_out,
-    scalars_out,
+    flat_mom_out,
+    flat_sec_out,
+    flat_ema_out,
+    loss_out,
+    norm_out,
+    both_ref,
 ):
     me = lax.axis_index("pts")
     grads = grads_ref[...]
     line, lane = divmod(FLAT, LANES)
     place_row = rows_of(256, LANES)
     at_loss = (place_row == 160 + line) & (lanes_of(256, LANES) == lane)
-    loss = jnp.sum(jnp.where(at_loss, grads, 0.0))
+    loss = jnp.where(at_loss, grads, 0.0)
+    loss_out[...] = jnp.sum(jnp.sum(loss, axis=0, keepdims=True), axis=1, keepdims=True)
     cleaned = jnp.where(at_loss, 0.0, grads)
     squares = jnp.sum(jnp.sum(cleaned * cleaned, axis=0, keepdims=True), axis=1, keepdims=True)
     norm = jnp.sqrt(squares)
+    norm_out[...] = norm
     factor = jnp.minimum(1.0, CLIP_NORM / norm)
-    flat_out[...] = cleaned[160:216] * factor
-    at = lanes_of(8, LANES)
-    scalars_out[...] = jnp.where(at == 0, loss, jnp.where(at == 1, norm, 0.0))
+    count = jnp.full((1, 1), step_ref[0].astype(F32), F32)
+    one_scale = 1.0 - jnp.exp(count * math.log(BETA_ONE))
+    two_scale = 1.0 - jnp.exp(count * math.log(BETA_TWO))
+    lines = FLAT_ROWS - 8
+
+    def as_line(values):
+        return jnp.broadcast_to(values, (lines, LANES)).reshape(lines * LANES)[0:FLAT]
+
+    flat_grad = (cleaned[160 : 160 + lines] * factor).reshape(lines * LANES)[0:FLAT]
+    flat_mom = BETA_ONE * flat_mom_ref[...] + (1.0 - BETA_ONE) * flat_grad
+    flat_sec = BETA_TWO * flat_sec_ref[...] + (1.0 - BETA_TWO) * flat_grad * flat_grad
+    flat_scaled = flat_mom / as_line(one_scale) / (jnp.sqrt(flat_sec / as_line(two_scale)) + ADAM_EPS)
+    flat_new = flat_ref[...] - LEARN_RATE * (flat_scaled + WEIGHT_DECAY * flat_ref[...])
+    flat_out[...] = flat_new
+    flat_mom_out[...] = flat_mom
+    flat_sec_out[...] = flat_sec
+    flat_ema_out[...] = EMA_KEEP * flat_ema_ref[...] + (1.0 - EMA_KEEP) * flat_new
     folded = cleaned[128:160]
     stacked = [
         cleaned[0:64, 0:64],
@@ -965,15 +1061,12 @@
         grad = grad + flag * stacked[position]
         owned = owned + flag
     grad = grad * factor
-    count = jnp.full((1, 1), step_ref[0].astype(F32), F32)
-    one_scale = 1.0 - jnp.exp(count * math.log(BETA_ONE))
-    two_scale = 1.0 - jnp.exp(count * math.log(BETA_TWO))
     basis_l = basis_l_ref[...]
     basis_r = basis_r_ref[...]
     left_new = BETA_TWO * left_ref[...] + (1.0 - BETA_TWO) * exact(grad, grad, ((1,), (1,)))
     right_new = BETA_TWO * right_ref[...] + (1.0 - BETA_TWO) * exact(grad, grad, ((0,), (0,)))
     both = orthonormal_pair(
-        jnp.concatenate([exact(left_new, basis_l), exact(right_new, basis_r)], 1)
+        jnp.concatenate([exact(left_new, basis_l), exact(right_new, basis_r)], 1), both_ref
     )
     basis_l_new = both[:, 0:C1]
     basis_r_new = both[:, C1 : 2 * C1]
@@ -997,18 +1090,6 @@
     basis_l_out[...] = jnp.where(held, basis_l_new, 0.0)
     basis_r_out[...] = jnp.where(held, basis_r_new, 0.0)
     average_out[...] = jnp.where(held, average_new, 0.0)
-
-
-def adam_update(weight, grad, first, second, average, count):
-    first_new = BETA_ONE * first + (1.0 - BETA_ONE) * grad
-    second_new = BETA_TWO * second + (1.0 - BETA_TWO) * grad * grad
-    scaled = (
-        first_new
-        / (1.0 - BETA_ONE**count)
-        / (jnp.sqrt(second_new / (1.0 - BETA_TWO**count)) + ADAM_EPS)
-    )
-    weight_new = weight - LEARN_RATE * (scaled + WEIGHT_DECAY * weight)
-    return (weight_new, first_new, second_new, EMA_KEEP * average + (1.0 - EMA_KEEP) * weight_new)
 
 
 def local(
@@ -1045,7 +1126,6 @@
     edges = NEIGH * half
     parts = coarse // LOW_B
     my_parts = parts // n_sub
-    flat2 = jnp.pad(flat, (0, FLAT_ROWS * LANES - FLAT)).reshape(FLAT_ROWS, LANES)
     vmem = pl.BlockSpec(memory_space=pltpu.VMEM)
     smem = pl.BlockSpec(memory_space=pltpu.SMEM)
     dma = pltpu.SemaphoreType.DMA
@@ -1059,6 +1139,8 @@
         VMEM((NEIGH, coarse), I32),
         pltpu.SMEM((NMATS,), I32),
         VMEM((C1, C1), F32),
+        VMEM((FLAT,), F32),
+        VMEM((FLAT_ROWS, LANES), F32),
         VMEM((16, fine), F32),
         VMEM((n_pts * 16, cap), F32),
         VMEM((n_pts, 16, cap), BF16),
@@ -1121,12 +1203,12 @@
         dma((n_pts,)),
         dma((8,)),
         dma((8,)),
-        dma((9,)),
+        dma((10,)),
     ]
     reduced = pl.pallas_call(
         functools.partial(main_kernel, n_pts, n_sub),
         out_shape=jax.ShapeDtypeStruct((256, LANES), F32),
-        in_specs=[pl.BlockSpec(memory_space=pltpu.HBM)] * 9 + [vmem],
+        in_specs=[pl.BlockSpec(memory_space=pltpu.HBM)] * 10,
         out_specs=vmem,
         scratch_shapes=scratch,
         compiler_params=pltpu.CompilerParams(
@@ -1142,18 +1224,17 @@
         coarse_nbr.T,
         owner,
         mats[0],
-        flat2,
+        flat,
     )
     square = jax.ShapeDtypeStruct((C1, C1), F32)
+    line = jax.ShapeDtypeStruct((FLAT,), F32)
+    single = jax.ShapeDtypeStruct((1, 1), F32)
     results = pl.pallas_call(
         soap_kernel,
-        out_shape=[square] * 8
-        + [
-            jax.ShapeDtypeStruct((56, LANES), F32),
-            jax.ShapeDtypeStruct((8, LANES), F32),
-        ],
-        in_specs=[vmem] + [smem] * 2 + [vmem] * 8,
-        out_specs=[vmem] * 10,
+        out_shape=[square] * 8 + [line] * 4 + [single] * 2,
+        in_specs=[vmem] + [smem] * 2 + [vmem] * 12,
+        out_specs=[vmem] * 14,
+        scratch_shapes=[VMEM((C1, 2 * C1), F32)],
     )(
         reduced,
         owner,
@@ -1166,13 +1247,13 @@
         mats_basis_l[0],
         mats_basis_r[0],
         mats_ema[0],
+        flat,
+        flat_mom,
+        flat_sec,
+        flat_ema,
     )
-    flat_grad = results[8].reshape(-1)[:FLAT]
-    count = step[0].astype(F32)
-    flat_out = adam_update(flat, flat_grad, flat_mom, flat_sec, flat_ema, count)
-    return (results[9][0, 0], results[9][0, 1]) + flat_out + tuple(
-        result[None] for result in results[:8]
-    )
+    scalars = (results[12].reshape(()), results[13].reshape(()))
+    return scalars + tuple(results[8:12]) + tuple(result[None] for result in results[:8])
 
 
 def solution(mesh):
@@ -1191,10 +1272,16 @@
         P(),
         P(),
     ) + (P("pts", None, None),) * 8
-    return jax.shard_map(
+    mapped = jax.shard_map(
         local,
         mesh=mesh,
         in_specs=placed,
         out_specs=(P(),) * 6 + (P("pts", None, None),) * 8,
         check_vma=False,
     )
+
+    def run(*arrays):
+        with jax.sharding.use_abstract_mesh(mesh.abstract_mesh):
+            return mapped(*arrays)
+
+    return run

time: 66.9 us -> 59.3 us (0.89)
  Pallas kernels: 60.9 us -> 57.6 us
  local copies, waits for them, and re-layouts: 2.73 us -> 0 us
  other arithmetic: 1.4 us -> 0 us
    pallas_call x1, Pallas kernels: 51.5 us -> 49.8 us  [local(): pl.pallas_call(functools.partial(main_kernel, n_pts, n_sub), out_shape=ja...]
    pallas_call x1, Pallas kernels: 9.33 us -> 7.83 us  [local(): pl.pallas_call(soap_kernel, out_shape=[square] * 8 + [line] * 4 + [single...]
    add x1 -> x0, other arithmetic: 1.4 us -> none  [adam_update(): EMA_KEEP * average + (1.0 - EMA_KEEP) * weight_new]
    reshape x1 -> x0, local copies, waits for them, and re-layouts: 1.37 us -> none  [local(): jnp.pad(flat, (0, FLAT_ROWS * LANES - FLAT)).reshape(FLAT_ROWS, LANES)]
    slice x1 -> x0, local copies, waits for them, and re-layouts: 1.34 us -> none  [local(): results[9][0, 1]]
where the time goes in v4:
time: 59.3 us; the launch traced here: 59.1 us
  Pallas kernels  57.6 us (97%)
  between operations  1.46 us (2%)
    pallas_call x1, Pallas kernels, local(): pl.pallas_call(functools.partial(main_kernel, n_pts, n_sub), out_shape=ja...  49.8 us
    pallas_call x1, Pallas kernels, local(): pl.pallas_call(soap_kernel, out_shape=[square] * 8 + [line] * 4 + [single...  7.83 us

profile of v4, /device:TPU:0, one launch (start us, length us, event | category | flops | bytes accessed | tf_op | source)
XLA Modules:
  0.0 59.1 jit_solution(13926556782657416496)
XLA Ops:
  1.3 49.8 %shard_map.308.grads_ref = f32[256,128]{1,0:T(8,128)} custom-call(bf16[6,2048]{1,0:T(8,128)(2,1)} %bitcast.29, s32[1,2048]{1,0:T(1,128)} %bitcast.38, s32[1,2048]{1,0:T(1,128)} %bitcast.39, s32[3,2048]{1,0:T(4,128)} %bitcast.30, s32[16,1024]{1,0:T(8,128)} %bitcast.27, s32[1,1024]{1,0:T(1,128)} %bitcast.40, s32[16,1024]{1,0:T(8,128)} %bitcast.28, ...), custom_call_target="tpu_custom_call" | custom-call | tf_op jit(solution)/shard_map/pallas_call | solution.py:1208
  51.1 7.8 %shard_map.309 = (f32[64,64]{1,0:T(8,128)}, f32[64,64]{1,0:T(8,128)}, f32[64,64]{1,0:T(8,128)}, f32[64,64]{1,0:T(8,128)}, f32[64,64]{1,0:T(8,128)}, /*index=5*/f...) custom-call(f32[256,128]{1,0:T(8,128)} %shard_map.308.grads_ref, ...), custom_call_target="tpu_custom_call" | custom-call | tf_op jit(solution)/shard_map/pallas_call | solution.py:1232

commit v5 on v4

--- a/solution.py
+++ b/solution.py
@@ -34,7 +34,7 @@
 LANES = 128
 FLAT_ROWS = 64
 LOW_B = 256
-CH = 80
+CH = 72
 NEG = -1e30
 
 
@@ -96,6 +96,14 @@
 def onehot(low, count):
     hit = rows_of(count, low.shape[1]) == low
     return jnp.where(hit, 1.0, 0.0).astype(BF16)
+
+
+def stored_onehot(low, iota):
+    count, length = iota.shape[0], low.shape[1]
+    wanted = jnp.broadcast_to(low.astype(F32), (16, length)).astype(BF16)
+    held = jnp.concatenate([iota] * (length // LANES), 1).reshape(count // 16, 16, length)
+    hit = held == wanted[None]
+    return jnp.where(hit, jnp.ones((), BF16), jnp.zeros((), BF16)).reshape(count, length)
 
 
 def pick(spread, high, parts):
@@ -180,6 +188,7 @@
     mats_ref,
     flat_line,
     flat_ref,
+    iota_ref,
     data,
     sacc,
     sendb,
@@ -303,6 +312,7 @@
             device_id_type=MESH,
         )
 
+    iota_ref[...] = rows_of(LOW_B, LANES).astype(F32).astype(BF16)
     for load in loads[0:5] + loads[9:]:
         load.wait()
     data[0:6, :] = pts_ref[...].astype(F32)
@@ -503,15 +513,14 @@
     lax.fori_loop(0, C1 // 8, log_sum, 0, unroll=2)
 
     def table_rows(values, target):
+        rows = []
         for part in range(my_parts):
             lanes = slice(part * LOW_B, (part + 1) * LOW_B)
-            stacked = jnp.concatenate(
-                [values[:, lanes], centre[:, lanes], jnp.zeros((8, LOW_B), F32)], 0
-            )
-            target[sub * my_parts + part] = stacked.astype(BF16)
+            rows = rows + [values[:, lanes], centre[:, lanes]]
+        target[sub] = jnp.concatenate(rows, 0).astype(BF16)
 
     table_rows(pooled_ref[...], ctab)
-    my_ctab = ctab.at[pl.ds(sub * my_parts, my_parts)]
+    my_ctab = ctab.at[sub]
     give_pooled = sibling(1, my_ctab, my_ctab)
     give_pooled.start()
 
@@ -569,7 +578,7 @@
 
     def attend_gather(k, lanes):
         index = cnbr_ref[pl.ds(k, 1), pl.ds(half_at, half)]
-        hot = onehot(index & (LOW_B - 1), LOW_B)
+        hot = stored_onehot(index & (LOW_B - 1), iota_ref[...])
         ohs[:, lanes] = hot
         high = lax.shift_right_logical(index, low_shift)
         found = pick(dot(ctab[...].reshape(parts * CH, LOW_B), hot), high, parts)
@@ -593,7 +602,7 @@
     def attend_score(k, lanes):
         sc[:, lanes] = dot(w_att2_t, est[128:144, lanes]) + b_att2
 
-    every_edge(attend_gather, 4)
+    every_edge(attend_gather, 16)
     every_edge(attend_pos, 16)
     every_edge(attend_edge, 16)
     every_edge(attend_act, 16)
@@ -621,7 +630,7 @@
     block = pooled_ref[...] + dot(w_out_t, mixed_ref[...].astype(BF16))
     blk_ref[...] = block
     table_rows(block, btab)
-    my_btab = btab.at[pl.ds(sub * my_parts, my_parts)]
+    my_btab = btab.at[sub]
     give_block = sibling(2, my_btab, my_btab)
     give_block.start()
 
@@ -631,7 +640,7 @@
 
     def fine_hot(j, lanes):
         for i in range(3):
-            foh[i, :, lanes] = onehot(source_of(lanes, i)[0], LOW_B)
+            foh[i, :, lanes] = stored_onehot(source_of(lanes, i)[0], iota_ref[...])
 
     every_slot(fine_hot, 2)
     give_block.wait_recv()
@@ -688,7 +697,7 @@
     loss = lax.fori_loop(0, slots // span, fine_loss, jnp.zeros((1, span), F32), unroll=4)
     every_slot(fine_fused, 8)
     dcp[...] = jnp.zeros_like(dcp)
-    every_slot(fine_scatter, 2)
+    every_slot(fine_scatter, 4)
 
     other = (1 - sub) * my_parts
     own = sub * my_parts
@@ -975,8 +984,12 @@
     errors = [departure(half) for half in halves]
     worst = jnp.max(jnp.maximum(jnp.abs(errors[0]), jnp.abs(errors[1])))
     halves = [correct(half, error) for half, error in zip(halves, errors)]
-    halves = [correct(half, departure(half)) for half in halves]
     both_ref[...] = jnp.concatenate(halves, 1)
+
+    @pl.when(worst > 1e-4)
+    def _():
+        again = [both_ref[:, 0:size], both_ref[:, size : 2 * size]]
+        both_ref[...] = jnp.concatenate([correct(half, departure(half)) for half in again], 1)
 
     @pl.when(jnp.logical_not(worst < 0.01))
     def _():
@@ -1141,6 +1154,7 @@
         VMEM((C1, C1), F32),
         VMEM((FLAT,), F32),
         VMEM((FLAT_ROWS, LANES), F32),
+        VMEM((LOW_B, LANES), BF16),
         VMEM((16, fine), F32),
         VMEM((n_pts * 16, cap), F32),
         VMEM((n_pts, 16, cap), BF16),
@@ -1153,8 +1167,8 @@
         VMEM((48, edges), BF16),
         VMEM((C1, half), F32),
         VMEM((C1, half), F32),
-        VMEM((parts, CH, LOW_B), BF16),
-        VMEM((parts, CH, LOW_B), BF16),
+        VMEM((n_sub, my_parts * CH, LOW_B), BF16),
+        VMEM((n_sub, my_parts * CH, LOW_B), BF16),
         VMEM((C1, edges), BF16),
         VMEM((144, edges), BF16),
         VMEM((144, edges), BF16),

time: 59.3 us -> 56.4 us (0.951)
  Pallas kernels: 57.6 us -> 54.7 us
    pallas_call x1, Pallas kernels: 49.8 us -> 47.4 us  [local(): pl.pallas_call(functools.partial(main_kernel, n_pts, n_sub), out_shape=ja...]
where the time goes in v5:
time: 56.4 us; the launch traced here: 56.2 us
  Pallas kernels  54.7 us (97%)
  between operations  1.46 us (3%)
    pallas_call x1, Pallas kernels, local(): pl.pallas_call(functools.partial(main_kernel, n_pts, n_sub), out_shape=ja...  47.4 us
    pallas_call x1, Pallas kernels, local(): pl.pallas_call(soap_kernel, out_shape=[square] * 8 + [line] * 4 + [single...  7.29 us

profile of v5, /device:TPU:0, one launch (start us, length us, event | category | flops | bytes accessed | tf_op | source)
XLA Modules:
  0.0 56.2 jit_solution(3287690551589739816)
XLA Ops:
  1.3 47.4 %shard_map.308.grads_ref = f32[256,128]{1,0:T(8,128)} custom-call(bf16[6,2048]{1,0:T(8,128)(2,1)} %bitcast.29, s32[1,2048]{1,0:T(1,128)} %bitcast.38, s32[1,2048]{1,0:T(1,128)} %bitcast.39, s32[3,2048]{1,0:T(4,128)} %bitcast.30, s32[16,1024]{1,0:T(8,128)} %bitcast.27, s32[1,1024]{1,0:T(1,128)} %bitcast.40, s32[16,1024]{1,0:T(8,128)} %bitcast.28, ...), custom_call_target="tpu_custom_call" | custom-call | tf_op jit(solution)/shard_map/pallas_call | solution.py:1222
  48.7 7.3 %shard_map.309 = (f32[64,64]{1,0:T(8,128)}, f32[64,64]{1,0:T(8,128)}, f32[64,64]{1,0:T(8,128)}, f32[64,64]{1,0:T(8,128)}, f32[64,64]{1,0:T(8,128)}, /*index=5*/f...) custom-call(f32[256,128]{1,0:T(8,128)} %shard_map.308.grads_ref, ...), custom_call_target="tpu_custom_call" | custom-call | tf_op jit(solution)/shard_map/pallas_call | solution.py:1246

commit v6 on v5

--- a/solution.py
+++ b/solution.py
@@ -694,7 +694,7 @@
 
     every_slot(fine_gather, 8)
     every_slot(fine_join, 8)
-    loss = lax.fori_loop(0, slots // span, fine_loss, jnp.zeros((1, span), F32), unroll=4)
+    loss = lax.fori_loop(0, slots // span, fine_loss, jnp.zeros((1, span), F32), unroll=8)
     every_slot(fine_fused, 8)
     dcp[...] = jnp.zeros_like(dcp)
     every_slot(fine_scatter, 4)
@@ -783,11 +783,20 @@
         jnp.add,
         [gst[128:144, k * half : (k + 1) * half].astype(F32)[0:8] for k in range(NEIGH)],
     )
-    w_att1_exact = w1[0:C1, 0:16].astype(BF16).astype(F32)[:, 0:8]
-    dqueries = exact(w_att1_exact, ds1_total)
+    w_att1_thrice = jnp.concatenate(
+        [w1[0:C1, 0:8]] * 3 + [jnp.zeros((C1, 8), F32)], 1
+    ).astype(BF16)
+
+    def three_parts(values):
+        high = values.astype(BF16).astype(F32)
+        middle = (values - high).astype(BF16).astype(F32)
+        low = values - high - middle
+        return jnp.concatenate([high, middle, low, jnp.zeros_like(low)], 0).astype(BF16)
+
+    dqueries = dot(w_att1_thrice, three_parts(ds1_total))
     give_dkv.wait_recv()
     dkv = own_half(dkp, dkr)
-    dkeys = -exact(w_att1_exact, dkv[C1 : C1 + 8])
+    dkeys = -dot(w_att1_thrice, three_parts(dkv[C1 : C1 + 8]))
     dqkv_low = jnp.concatenate([dqueries, dkeys, dkv[0:C1]], 0).astype(BF16)
     gbuf[...] = jnp.zeros_like(gbuf)
     gbuf[0:64, :] = dot_nt(pooled_ref[...].astype(BF16), dqkv_low[0:128])
@@ -1073,11 +1082,13 @@
         flag = jnp.where(owner_ref[position] == me, 1.0, 0.0)
         grad = grad + flag * stacked[position]
         owned = owned + flag
+    raw = grad
+    scale = (1.0 - BETA_TWO) * (factor * factor)
     grad = grad * factor
     basis_l = basis_l_ref[...]
     basis_r = basis_r_ref[...]
-    left_new = BETA_TWO * left_ref[...] + (1.0 - BETA_TWO) * exact(grad, grad, ((1,), (1,)))
-    right_new = BETA_TWO * right_ref[...] + (1.0 - BETA_TWO) * exact(grad, grad, ((0,), (0,)))
+    left_new = BETA_TWO * left_ref[...] + scale * exact(raw, raw, ((1,), (1,)))
+    right_new = BETA_TWO * right_ref[...] + scale * exact(raw, raw, ((0,), (0,)))
     both = orthonormal_pair(
         jnp.concatenate([exact(left_new, basis_l), exact(right_new, basis_r)], 1), both_ref
     )

time: 56.4 us -> 55.8 us (0.989)
  Pallas kernels: 54.7 us -> 54.1 us
where the time goes in v6:
time: 55.8 us; the launch traced here: 55.6 us
  Pallas kernels  54.1 us (97%)
  between operations  1.46 us (3%)
    pallas_call x1, Pallas kernels, local(): pl.pallas_call(functools.partial(main_kernel, n_pts, n_sub), out_shape=ja...  46.9 us
    pallas_call x1, Pallas kernels, local(): pl.pallas_call(soap_kernel, out_shape=[square] * 8 + [line] * 4 + [single...  7.23 us

profile of v6, /device:TPU:0, one launch (start us, length us, event | category | flops | bytes accessed | tf_op | source)
XLA Modules:
  0.0 55.6 jit_solution(10593474079222393783)
XLA Ops:
  1.3 46.9 %shard_map.308.grads_ref = f32[256,128]{1,0:T(8,128)} custom-call(bf16[6,2048]{1,0:T(8,128)(2,1)} %bitcast.29, s32[1,2048]{1,0:T(1,128)} %bitcast.38, s32[1,2048]{1,0:T(1,128)} %bitcast.39, s32[3,2048]{1,0:T(4,128)} %bitcast.30, s32[16,1024]{1,0:T(8,128)} %bitcast.27, s32[1,1024]{1,0:T(1,128)} %bitcast.40, s32[16,1024]{1,0:T(8,128)} %bitcast.28, ...), custom_call_target="tpu_custom_call" | custom-call | tf_op jit(solution)/shard_map/pallas_call | solution.py:1233
  48.2 7.2 %shard_map.309 = (f32[64,64]{1,0:T(8,128)}, f32[64,64]{1,0:T(8,128)}, f32[64,64]{1,0:T(8,128)}, f32[64,64]{1,0:T(8,128)}, f32[64,64]{1,0:T(8,128)}, /*index=5*/f...) custom-call(f32[256,128]{1,0:T(8,128)} %shard_map.308.grads_ref, ...), custom_call_target="tpu_custom_call" | custom-call | tf_op jit(solution)/shard_map/pallas_call | solution.py:1257

commit v7 on v6

--- a/solution.py
+++ b/solution.py
@@ -430,11 +430,18 @@
     forward.start()
     for source in range(n_pts):
         slot[:, source * cap : (source + 1) * cap] = recv[sub * n_pts + source].astype(F32)
+
+    def fill_table(side):
+        came = recv[pl.ds(side * n_pts, n_pts)].astype(F32)
+        rows = n_pts * 8
+        ones_row = (rows_of(rows, cap) & 7) == 7
+        filled = jnp.where(ones_row, 1.0, came[:, 0:8, :].reshape(rows, cap))
+        tabb[pl.ds(pl.multiple_of(side * rows, rows), rows), :] = filled.astype(BF16)
+
+    fill_table(sub)
     forward.wait_recv()
 
-    table = recv[...].astype(F32)[:, 0:8, :].reshape(sources * 8, cap)
-    ones_row = (rows_of(sources * 8, cap) & 7) == 7
-    tabb[...] = jnp.where(ones_row, 1.0, table).astype(BF16)
+    fill_table(1 - sub)
     count_row = jnp.sum(recv[...].astype(F32)[:, 8:16, :], axis=0)[7:8, 0:32]
     count_at = jnp.broadcast_to(count_row, (16, 32))
     low_hit = lanes_of(16, 32) == rows_of(16, 32)
@@ -450,7 +457,7 @@
     )
 
     def gather_points(index):
-        hot = onehot(index & (cap - 1), cap)
+        hot = stored_onehot(index & (cap - 1), iota_ref[0:cap, :])
         high = jnp.broadcast_to(lax.shift_right_logical(index, shift), (8, index.shape[1]))
         return pick(dot(tabb[...], hot), high, sources)
 
@@ -642,7 +649,7 @@
         for i in range(3):
             foh[i, :, lanes] = stored_onehot(source_of(lanes, i)[0], iota_ref[...])
 
-    every_slot(fine_hot, 2)
+    every_slot(fine_hot, 1)
     give_block.wait_recv()
 
     def fine_gather(j, lanes):

time: 55.8 us -> 55.6 us (level)
  no operation moved by 1% of the time
where the time goes in v7:
time: 55.6 us; the launch traced here: 55.4 us
  Pallas kernels  54 us (97%)
  between operations  1.46 us (3%)
    pallas_call x1, Pallas kernels, local(): pl.pallas_call(functools.partial(main_kernel, n_pts, n_sub), out_shape=ja...  46.7 us
    pallas_call x1, Pallas kernels, local(): pl.pallas_call(soap_kernel, out_shape=[square] * 8 + [line] * 4 + [single...  7.24 us

profile of v7, /device:TPU:0, one launch (start us, length us, event | category | flops | bytes accessed | tf_op | source)
XLA Modules:
  0.0 55.4 jit_solution(16947137894945926903)
XLA Ops:
  1.3 46.7 %shard_map.308.grads_ref = f32[256,128]{1,0:T(8,128)} custom-call(bf16[6,2048]{1,0:T(8,128)(2,1)} %bitcast.29, s32[1,2048]{1,0:T(1,128)} %bitcast.38, s32[1,2048]{1,0:T(1,128)} %bitcast.39, s32[3,2048]{1,0:T(4,128)} %bitcast.30, s32[16,1024]{1,0:T(8,128)} %bitcast.27, s32[1,1024]{1,0:T(1,128)} %bitcast.40, s32[16,1024]{1,0:T(8,128)} %bitcast.28, ...), custom_call_target="tpu_custom_call" | custom-call | tf_op jit(solution)/shard_map/pallas_call | solution.py:1240
  48.0 7.2 %shard_map.309 = (f32[64,64]{1,0:T(8,128)}, f32[64,64]{1,0:T(8,128)}, f32[64,64]{1,0:T(8,128)}, f32[64,64]{1,0:T(8,128)}, f32[64,64]{1,0:T(8,128)}, /*index=5*/f...) custom-call(f32[256,128]{1,0:T(8,128)} %shard_map.308.grads_ref, ...), custom_call_target="tpu_custom_call" | custom-call | tf_op jit(solution)/shard_map/pallas_call | solution.py:1264
